TPU v7x, 128 devices: a whole 4x4x4 slice. The times are simulated.
128 devices in a mesh: shard: 8 (over z_lo, y), ctx: 16 (over x, z_hi, core).
Axes of the slice: x: 4, y: 4, z: 4 (z_hi: 2, z_lo: 2; z = z_hi * 2 + z_lo), core: 2. Of those that a mesh axis runs over, the one named last changes fastest.
Arguments:
- tokens: bfloat16 [32768, 960], P(('shard', 'ctx')), may hold values from -6 to 6
- w_query: bfloat16 [960, 960], P('shard', 'ctx'), may hold values from -0.1875 to 0.1875
- w_key: bfloat16 [960, 320], P('shard', 'ctx'), may hold values from -0.1875 to 0.1875
- w_value: bfloat16 [960, 320], P('shard', 'ctx'), may hold values from -0.1875 to 0.1875
- w_out: bfloat16 [960, 960], P('shard', 'ctx'), may hold values from -1.5 to 1.5
- w_gate: bfloat16 [960, 2560], P('shard', 'ctx'), may hold values from -0.1875 to 0.1875
- w_up: bfloat16 [960, 2560], P('shard', 'ctx'), may hold values from -0.1875 to 0.1875
- w_down: bfloat16 [2560, 960], P('shard', 'ctx'), may hold values from -0.125 to 0.125
- attention_norm_gain: float32 [960], replicated, may hold values from 0.1 to 1.9
- feedforward_norm_gain: float32 [960], replicated, may hold values from 0.1 to 1.9
- span_order: int32 [8, 32], P('shard'), may hold values from 0 to 31, as said below
- positions: int32 [8, 4096], P('shard'), may hold values from 0 to 8191, as said below
- out_grad: bfloat16 [32768, 960], P(('shard', 'ctx')), may hold values from -6 to 6
Outputs:
- output: bfloat16 [32768, 960], P(('shard', 'ctx'))
- input_grad: bfloat16 [32768, 960], P(('shard', 'ctx'))
- grad_query: float32 [960, 960], P('shard', 'ctx')
- grad_key: float32 [960, 320], P('shard', 'ctx')
- grad_value: float32 [960, 320], P('shard', 'ctx')
- grad_out: float32 [960, 960], P('shard', 'ctx')
- grad_gate: float32 [960, 2560], P('shard', 'ctx')
- grad_up: float32 [960, 2560], P('shard', 'ctx')
- grad_down: float32 [2560, 960], P('shard', 'ctx')
- grad_norm_attn: float32 [960], replicated
- grad_norm_mlp: float32 [960], replicated
Inputs may be any that keep to these rules, and one draw needn't show every extreme that they name: `span_order`: each row is a permutation of the 32 blocks of one sequence; ctx index c holds blocks row[2c] then row[2c + 1], and row[2c] + row[2c + 1] = 31. `positions`: each row starts at 0, rises strictly by 1 to 3 from one token to the next, and ends at 8191.
All inputs are finite; a program needn't handle non-finite values.
Results may differ from a plain program's by a relative error of at most 0.028.
Values may be sent and summed in bfloat16 or wider, within the bound.
No kernel may reach another device: no remote copies, remote signals or barrier semaphores. Data moves between devices by JAX's collectives and lax.ppermute only.
A program may use at most 256 MiB of HBM per device.

v0:
```python
import jax
import jax.numpy as jnp
from jax import lax
from jax.sharding import PartitionSpec as P

D = 960
HEADS = 15
KV_HEADS = 5
HEAD_DIM = 64


EPS = 1e-05
ROPE_BASE = 100000.0


def sent_together(arrays, axis, dim, along):
    widths = [a.shape[along] for a in arrays]
    both = jnp.concatenate(arrays, axis=along)
    result = lax.all_gather(both, axis, axis=dim, tiled=True)
    return tuple(jnp.split(result, [sum(widths[:k]) for k in range(1, len(widths))], axis=along))


def side_by_side(arrays, axis, dim, along):
    ends, at = ([], 0)
    for a in arrays[:-1]:
        at += a.shape[along]
        ends.append(at)
    both = jnp.concatenate(arrays, axis=along)
    return tuple(
        jnp.split(lax.psum_scatter(both, axis, scatter_dimension=dim, tiled=True), ends, axis=along)
    )


def norm_forward_step(value, gain):
    inverse = lax.rsqrt(jnp.mean(value * value, axis=-1, keepdims=True) + EPS)
    normed = value * inverse
    return (normed, inverse, (normed * gain).astype(jnp.bfloat16))


def norm_gradient_step(grad_norm, normed, inverse, gain):
    scaled = grad_norm * gain
    inner = jnp.mean(scaled * normed, axis=-1, keepdims=True)
    return (inverse * (scaled - normed * inner), jnp.sum(grad_norm * normed, axis=0))


def rotate(value, cosine, sine):
    half_dim = value.shape[-1] // 2
    first = value[..., :half_dim]
    second = value[..., half_dim:]
    return jnp.concatenate(
        [first * cosine - second * sine, second * cosine + first * sine], axis=-1
    )


def unrotate(value, cosine, sine):
    half_dim = value.shape[-1] // 2
    first = value[..., :half_dim]
    second = value[..., half_dim:]
    return jnp.concatenate(
        [first * cosine + second * sine, second * cosine - first * sine], axis=-1
    )


def outer_sum(left, right):
    return jnp.einsum("ti,tj->ij", left, right, preferred_element_type=jnp.float32)


def back_dot(left, weight):
    return jnp.einsum("ti,ji->tj", left, weight, preferred_element_type=jnp.float32)


def body(
    tokens,
    w_query,
    w_key,
    w_value,
    w_out,
    w_gate,
    w_up,
    w_down,
    attention_norm_gain,
    feedforward_norm_gain,
    span_order,
    positions,
    out_grad,
):
    rows = tokens.shape[0]
    half_rows = rows // 2
    group = HEADS // KV_HEADS
    kv_width = KV_HEADS * HEAD_DIM
    scale = HEAD_DIM ** (-0.5)
    me = lax.axis_index("ctx")
    order = span_order[0]
    slot_ids = jnp.arange(order.shape[0], dtype=jnp.int32)

    def sequence_rows(global_rows):
        device = global_rows // rows
        within = global_rows % rows
        slot = 2 * device + within // half_rows
        span = jnp.sum(jnp.where(slot[:, None] == slot_ids[None, :], order[None, :], 0), axis=1)
        return span * half_rows + within % half_rows

    query_index = sequence_rows(me * rows + jnp.arange(rows, dtype=jnp.int32))
    place = jnp.concatenate(
        [
            lax.dynamic_slice_in_dim(positions[0], query_index[0], half_rows, 0),
            lax.dynamic_slice_in_dim(positions[0], query_index[half_rows], half_rows, 0),
        ]
    )
    half_dim = HEAD_DIM // 2
    freq = jnp.power(ROPE_BASE, -jnp.arange(half_dim, dtype=jnp.float32) / half_dim)
    angle = place.astype(jnp.float32)[:, None] * freq[None, :]
    cosine = jnp.cos(angle)[:, None, :]
    sine = jnp.sin(angle)[:, None, :]
    row_part = (
        *sent_together((w_query, w_key, w_value, w_out, w_gate, w_up), "shard", 0, 1),
        lax.all_gather(w_down, "shard", axis=0, tiled=True),
    )
    wq, wk, wv, wo, wg, wu, wd = (
        lax.all_gather(row_part[0], "ctx", axis=1, tiled=True),
        *sent_together((row_part[1], row_part[2]), "ctx", 1, 0),
        lax.all_gather(row_part[3], "ctx", axis=1, tiled=True),
        *sent_together((row_part[4], row_part[5]), "ctx", 1, 0),
        lax.all_gather(row_part[6], "ctx", axis=1, tiled=True),
    )
    layer_input_rows = tokens.astype(jnp.float32)
    first_unit_rows, first_inverse_norm, first_normed_rows = norm_forward_step(
        layer_input_rows, attention_norm_gain
    )
    query = jnp.dot(first_normed_rows, wq, preferred_element_type=jnp.float32)
    key_lin = jnp.dot(first_normed_rows, wk, preferred_element_type=jnp.float32)
    value = jnp.dot(first_normed_rows, wv, preferred_element_type=jnp.float32).astype(jnp.bfloat16)
    query_rot = rotate(query.reshape(rows, HEADS, HEAD_DIM), cosine, sine).astype(jnp.bfloat16)
    key_rot = rotate(key_lin.reshape(rows, KV_HEADS, HEAD_DIM), cosine, sine).astype(jnp.bfloat16)
    grouped = query_rot.reshape(rows, KV_HEADS, group, HEAD_DIM)
    kv_local = jnp.concatenate([key_rot.reshape(rows, kv_width), value], axis=1)

    def split_piece(piece):
        count = piece.shape[0]
        keys = piece[:, :kv_width].reshape(count, KV_HEADS, HEAD_DIM)
        values = piece[:, kv_width:].reshape(count, KV_HEADS, HEAD_DIM)
        key_index = sequence_rows(jnp.arange(count, dtype=jnp.int32))
        allowed = key_index[None, :] <= query_index[:, None]
        scores = (
            jnp.einsum("qgrd,kgd->qgrk", grouped, keys, preferred_element_type=jnp.float32) * scale
        )
        expo = jnp.where(allowed[:, None, None, :], jnp.exp(scores), 0.0)
        return (keys, values, expo)

    keys, values, expo = split_piece(lax.all_gather(kv_local, "ctx", axis=0, tiled=True))
    numer = jnp.einsum(
        "qgrk,kgd->qgrd", expo.astype(jnp.bfloat16), values, preferred_element_type=jnp.float32
    )
    numer, total = (numer, jnp.sum(expo, axis=-1))
    attended = numer / total[..., None]
    attended_low = attended.reshape(rows, D).astype(jnp.bfloat16)
    first_hidden_rows = layer_input_rows + jnp.dot(
        attended_low, wo, preferred_element_type=jnp.float32
    )
    second_unit_rows, second_inverse_norm, second_normed_rows = norm_forward_step(
        first_hidden_rows, feedforward_norm_gain
    )
    gate = jnp.dot(second_normed_rows, wg, preferred_element_type=jnp.float32)
    upward = jnp.dot(second_normed_rows, wu, preferred_element_type=jnp.float32)
    sigma = jax.nn.sigmoid(gate)
    silu_gate = gate * sigma
    active = (silu_gate * upward).astype(jnp.bfloat16)
    result = (first_hidden_rows + jnp.dot(active, wd, preferred_element_type=jnp.float32)).astype(
        jnp.bfloat16
    )
    dact = back_dot(out_grad, wd)
    dgate = (dact * upward * sigma * (1.0 + gate * (1.0 - sigma))).astype(jnp.bfloat16)
    dup = (dact * silu_gate).astype(jnp.bfloat16)
    second_normed_gradient = back_dot(dgate, wg) + back_dot(dup, wu)
    hidden_feedforward_gradient, feedforward_gain_gradient = norm_gradient_step(
        second_normed_gradient, second_unit_rows, second_inverse_norm, feedforward_norm_gain
    )
    dh_one = out_grad.astype(jnp.float32) + hidden_feedforward_gradient
    dh_low = dh_one.astype(jnp.bfloat16)
    dob = back_dot(dh_low, wo).astype(jnp.bfloat16)
    dob_heads = dob.reshape(rows, KV_HEADS, group, HEAD_DIM)
    dnum = (dob_heads.astype(jnp.float32) / total[..., None]).astype(jnp.bfloat16)
    delta = jnp.sum(dob_heads.astype(jnp.float32) * attended, axis=-1) / total
    piece = lax.all_gather(kv_local, "ctx", axis=0, tiled=True)
    keys, values, expo = split_piece(piece)
    count = piece.shape[0]
    dprob = jnp.einsum("qgrd,kgd->qgrk", dnum, values, preferred_element_type=jnp.float32)
    dscore = (expo * (dprob - delta[..., None])).astype(jnp.bfloat16)
    dq_sum = jnp.einsum("qgrk,kgd->qgrd", dscore, keys, preferred_element_type=jnp.float32) * scale
    dkey = jnp.einsum("qgrk,qgrd->kgd", dscore, grouped, preferred_element_type=jnp.float32) * scale
    dval = jnp.einsum(
        "qgrk,qgrd->kgd", expo.astype(jnp.bfloat16), dnum, preferred_element_type=jnp.float32
    )
    block = jnp.concatenate([dkey.reshape(count, kv_width), dval.reshape(count, kv_width)], axis=1)
    dkv_own = lax.psum_scatter(
        block.astype(jnp.bfloat16), "ctx", scatter_dimension=0, tiled=True
    ).astype(jnp.float32)
    dq_low = (
        unrotate(dq_sum.reshape(rows, HEADS, HEAD_DIM), cosine, sine)
        .reshape(rows, D)
        .astype(jnp.bfloat16)
    )
    dk_low = (
        unrotate(dkv_own[:, :kv_width].reshape(rows, KV_HEADS, HEAD_DIM), cosine, sine)
        .reshape(rows, kv_width)
        .astype(jnp.bfloat16)
    )
    dv_low = dkv_own[:, kv_width:].astype(jnp.bfloat16)
    first_normed_gradient = back_dot(dq_low, wq) + back_dot(dk_low, wk) + back_dot(dv_low, wv)
    attention_input_gradient, attention_gain_gradient = norm_gradient_step(
        first_normed_gradient, first_unit_rows, first_inverse_norm, attention_norm_gain
    )
    input_grad = (dh_one + attention_input_gradient).astype(jnp.bfloat16)
    col_sums = (
        lax.psum_scatter(
            outer_sum(first_normed_rows, dq_low).astype(jnp.bfloat16),
            "ctx",
            scatter_dimension=1,
            tiled=True,
        ).astype(jnp.float32),
        *tuple(
            (
                part.astype(jnp.float32)
                for part in side_by_side(
                    (
                        outer_sum(first_normed_rows, dk_low).astype(jnp.bfloat16),
                        outer_sum(first_normed_rows, dv_low).astype(jnp.bfloat16),
                    ),
                    "ctx",
                    1,
                    0,
                )
            )
        ),
        lax.psum_scatter(
            outer_sum(attended_low, dh_low).astype(jnp.bfloat16),
            "ctx",
            scatter_dimension=1,
            tiled=True,
        ).astype(jnp.float32),
        *tuple(
            (
                part.astype(jnp.float32)
                for part in side_by_side(
                    (
                        outer_sum(second_normed_rows, dgate).astype(jnp.bfloat16),
                        outer_sum(second_normed_rows, dup).astype(jnp.bfloat16),
                    ),
                    "ctx",
                    1,
                    0,
                )
            )
        ),
        lax.psum_scatter(
            outer_sum(active, out_grad).astype(jnp.bfloat16), "ctx", scatter_dimension=1, tiled=True
        ).astype(jnp.float32),
    )
    shards = (
        *tuple(
            (
                part.astype(jnp.float32)
                for part in side_by_side(
                    (
                        col_sums[0].astype(jnp.bfloat16),
                        col_sums[1].astype(jnp.bfloat16),
                        col_sums[2].astype(jnp.bfloat16),
                        col_sums[3].astype(jnp.bfloat16),
                        col_sums[4].astype(jnp.bfloat16),
                        col_sums[5].astype(jnp.bfloat16),
                    ),
                    "shard",
                    0,
                    1,
                )
            )
        ),
        lax.psum_scatter(
            col_sums[6].astype(jnp.bfloat16), "shard", scatter_dimension=0, tiled=True
        ).astype(jnp.float32),
    )
    gains = lax.psum((attention_gain_gradient, feedforward_gain_gradient), ("shard", "ctx"))
    return (
        result,
        input_grad,
        shards[0],
        shards[1],
        shards[2],
        shards[3],
        shards[4],
        shards[5],
        shards[6],
        gains[0],
        gains[1],
    )


def solution(mesh):
    return jax.shard_map(
        body,
        mesh=mesh,
        in_specs=(
            P(("shard", "ctx"), None),
            P("shard", "ctx"),
            P("shard", "ctx"),
            P("shard", "ctx"),
            P("shard", "ctx"),
            P("shard", "ctx"),
            P("shard", "ctx"),
            P("shard", "ctx"),
            P(),
            P(),
            P("shard", None),
            P("shard", None),
            P(("shard", "ctx"), None),
        ),
        out_specs=(
            P(("shard", "ctx"), None),
            P(("shard", "ctx"), None),
            P("shard", "ctx"),
            P("shard", "ctx"),
            P("shard", "ctx"),
            P("shard", "ctx"),
            P("shard", "ctx"),
            P("shard", "ctx"),
            P("shard", "ctx"),
            P(),
            P(),
        ),
        check_vma=False,
    )
```

profile of v0, /device:TPU:1, one launch (start us, length us, event | category | flops | bytes accessed | tf_op | source)
XLA Modules:
  0.0 990.2 jit_solution(6659394494621538648)
XLA Ops:
  12.5 26.7 %all_gather.25 = bf16[960,480]{1,0:T(8,128)(2,1)S(1)} all-gather(bf16[120,480]{1,0:T(8,128)(2,1)S(1)} %concatenate.57), channel_id=1, replica_groups=mesh['shard'=8,'ctx'=16] {'shard'}, dimensions={0}, use_global_device_ids=true | all-gather | bytes 1036800 | tf_op jit(solution)/shard_map/all_gather | solution.py:19
  42.5 22.6 %all-gather.3 = bf16[8,320,60]{1,2,0:T(8,128)(2,1)S(1)} all-gather(bf16[1,320,60]{1,2,0:T(8,128)(2,1)S(1)} %bitcast.170), channel_id=1, replica_groups=mesh['shard'=8,'ctx'=16] {'shard'}, dimensions={0}, use_global_device_ids=true | all-gather | bytes 345600 | tf_op jit(solution)/shard_map/all_gather | solution.py:117
  72.1 21.9 %all-gather.16.cloned.1.call-done = bf16[16,20,1920]{2,1,0:T(8,128)(2,1)} async-done(((bf16[1,20,1920]{2,1,0:T(8,128)(2,1)}), bf16[16,20,1920]{2,1,0:T(8,128)(2,1)}) %all-gather.16.cloned.1.call-update) | async-done | bytes 1228816 | tf_op jit(solution)/shard_map/all_gather | solution.py:19
  103.0 40.4 %all-gather.20.cloned.1.call-done = bf16[16,60,960]{2,1,0:T(8,128)(2,1)} async-done(((bf16[1,60,960]{2,1,0:T(8,128)(2,1)}), bf16[16,60,960]{2,1,0:T(8,128)(2,1)}) %all-gather.20.cloned.1.call-update) | async-done | bytes 1843216 | tf_op jit(solution)/shard_map/all_gather | solution.py:122
  147.4 45.6 %all-gather.18.cloned.1.call-done = bf16[16,60,960]{2,1,0:T(8,128)(2,1)} async-done(((bf16[1,60,960]{2,1,0:T(8,128)(2,1)}), bf16[16,60,960]{2,1,0:T(8,128)(2,1)}) %all-gather.18.cloned.1.call-update) | async-done | bytes 1843216 | tf_op jit(solution)/shard_map/all_gather | solution.py:120
  197.4 57.0 %all-gather.22.cloned.1.call-done = bf16[16,60,2560]{2,1,0:T(8,128)(2,1)} async-done(((bf16[1,60,2560]{2,1,0:T(8,128)(2,1)}), bf16[16,60,2560]{2,1,0:T(8,128)(2,1)}) %all-gather.22.cloned.1.call-update) | async-done | bytes 4915216 | tf_op jit(solution)/shard_map/all_gather | solution.py:124
  254.4 7.3 reshape.343
  261.8 5.4 fusion.98
  267.2 52.9 %all-gather.12.cloned.1.call-done = bf16[4096,640]{0,1:T(8,128)(2,1)} async-done(((bf16[256,640]{0,1:T(8,128)(2,1)}), bf16[4096,640]{0,1:T(8,128)(2,1)}) %all-gather.12.cloned.1.call-update) | async-done | bytes 5242896 | tf_op jit(solution)/shard_map/all_gather | solution.py:150
  320.1 4.5 fusion.90
  324.6 25.2 %fusion.5 = (f32[256,5,3]{0,2,1:T(4,128)S(1)}, f32[5,4096,256,3]{2,1,3,0:T(8,128)}) fusion(pred[256,4096]{0,1:T(8,128)(4,1)} %broadcast_compare_fusion, bf16[4096,5,64,1]{0,2,3,1:T(8,128)(2,1)S(1)} %bitcast.140, bf16[256,5,3,32]{0,3,2,1:T(8,128)(2,1)} %bitcast.159, bf16[256,5,3,32]{0,3,2,1:T(8,128)(2,1)S(1)} %bitcast.157), kind=kOutput, calls=%fused_computation.4 | convolution fusion | flops 2061431040 | bytes 67091456 | tf_op jit(solution)/shard_map/qgrd,kgd->qgrk/dot_general | solution.py:145
  349.8 26.3 %fusion.97 = (bf16[256,5,3,64]{0,3,2,1:T(8,128)(2,1)S(1)}, f32[256,5,3,64]{0,3,2,1:T(8,128)}) fusion(f32[256,5,3]{0,2,1:T(4,128)S(1)} %get-tuple-element.115, bf16[4096,5,64,1]{0,2,3,1:T(8,128)(2,1)} %bitcast.150, f32[5,4096,256,3]{2,1,3,0:T(8,128)} %get-tuple-element.116, pred[256,4096]{0,1:T(8,128)(4,1)} %broadcast_compare_fusion), kind=kOutput, calls=%fused_computation.176 | convolution fusion | flops 2060943360 | bytes 68074496 | tf_op jit(solution)/shard_map/qgrk,kgd->qgrd/dot_general | solution.py:151
  378.0 21.5 %all-gather.14.cloned.1.call-done = bf16[1920,2560]{0,1:T(8,128)(2,1)} async-done(((bf16[1920,160]{0,1:T(8,128)(2,1)}), bf16[1920,2560]{0,1:T(8,128)(2,1)}) %all-gather.14.cloned.1.call-update) | async-done | bytes 9830416 | tf_op jit(solution)/shard_map/all_gather | solution.py:19
  399.6 5.7 fusion.12
  405.3 6.6 multiply_convert_fusion.1
  411.9 4.4 fusion.10
  421.4 23.9 %fusion.8 = bf16[5,64,4096]{2,1,0:T(8,128)(2,1)} fusion(f32[5,4096,256,3]{2,1,3,0:T(8,128)} %get-tuple-element.116, pred[256,4096]{0,1:T(8,128)(4,1)} %broadcast_compare_fusion, bf16[256,5,3,64]{0,3,2,1:T(8,128)(2,1)S(1)} %bitcast.153, f32[256,5,3]{0,2,1:T(4,128)S(1)} %get-tuple-element.115), kind=kOutput, calls=%fused_computation.13 | convolution fusion | flops 2062499840 | bytes 67091456 | tf_op jit(solution)/shard_map/qgrk,qgrd->kgd/dot_general | solution.py:191
  446.7 37.9 %fusion.4 = bf16[256,5,3,4096]{0,3,2,1:T(8,128)(2,1)} fusion(f32[5,4096,256,3]{2,1,3,0:T(8,128)} %get-tuple-element.116, bf16[4096,5,64,1]{0,2,3,1:T(8,128)(2,1)} %bitcast.151, f32[256,5,3]{0,2,1:T(4,128)S(1)} %div.109, pred[256,4096]{0,1:T(8,128)(4,1)} %broadcast_compare_fusion, bf16[256,5,3,64]{0,3,2,1:T(8,128)(2,1)S(1)} %bitcast.155, ...), kind=kOutput, calls=%fused_computation.2 | convolution fusion | flops 2092646400 | bytes 98564096 | tf_op jit(solution)/shard_map/qgrd,kgd->qgrk/dot_general | solution.py:187
  484.6 14.7 %fusion.9 = bf16[5,64,4096]{2,1,0:T(8,128)(2,1)S(1)} fusion(bf16[256,5,3,4096]{0,3,2,1:T(8,128)(2,1)} %fusion.4, bf16[256,5,3,32]{0,3,2,1:T(8,128)(2,1)} %bitcast.160, bf16[256,5,3,32]{0,3,2,1:T(8,128)(2,1)S(1)} %bitcast.158), kind=kOutput, calls=%fused_computation.14 | convolution fusion | flops 2016870400 | bytes 34570240 | tf_op jit(solution)/shard_map/qgrk,qgrd->kgd/dot_general | solution.py:190
  499.3 4.6 pad_maximum_fusion.1
  504.4 5.0 convolution_convert_fusion.1
  509.4 75.7 %reduce-scatter.15.cloned.1.call-done = bf16[256,640]{0,1:T(8,128)(2,1)} async-done(((bf16[4096,640]{0,1:T(8,128)(2,1)}), bf16[256,640]{0,1:T(8,128)(2,1)}) %reduce-scatter.15.cloned.1.call-update) | async-done | bytes 327696 | tf_op jit(solution)/shard_map/reduce_scatter | solution.py:195
  591.3 7.1 pad_maximum_fusion
  598.4 14.4 %copy.137 = bf16[1920,2560]{0,1:T(8,128)(2,1)} copy(bf16[1920,2560]{1,0:T(8,128)(2,1)} %pad_maximum_fusion) | data formatting | bytes 19660800
  612.8 12.9 %convolution_multiply_fusion = f32[5,64,256,3]{2,1,3,0:T(8,128)S(1)} fusion(bf16[4096,5,64,1]{0,2,3,1:T(8,128)(2,1)} %bitcast.141, bf16[256,5,3,4096]{0,3,2,1:T(8,128)(2,1)} %fusion.4), kind=kOutput, calls=%fused_computation.40 | convolution fusion | flops 2013511680 | bytes 35061760 | tf_op jit(solution)/shard_map/qgrk,kgd->qgrd/dot_general | solution.py:189
  633.7 121.3 %fusion.89 = (bf16[960,64]{0,1:T(8,128)(2,1)S(1)}, bf16[960,64]{0,1:T(8,128)(2,1)S(1)}, bf16[2560,64]{0,1:T(8,128)(2,1)S(1)}) fusion(bf16[960,960]{0,1:T(8,128)(2,1)} %convolution_convert_fusion.4, bf16[960,960]{0,1:T(8,128)(2,1)} %convolution_convert_fusion.3, bf16[2560,960]{0,1:T(8,128)(2,1)} %convolution_convert_fusion), kind=kCustom, calls=%all-reduce-scatter.3 | all-reduce-scatter fusion | flops 4587521 | bytes 9175552
  755.1 5.9 collective-permute-start.2
  769.4 6.2 collective-permute-start.1
  781.3 83.2 %reduce-scatter.19.cloned.1.call-done = bf16[160,1920]{1,0:T(8,128)(2,1)} async-done(((bf16[2560,1920]{1,0:T(8,128)(2,1)}), bf16[160,1920]{1,0:T(8,128)(2,1)}) %reduce-scatter.19.cloned.1.call-update) | async-done | bytes 614416
  873.3 5.1 fusion.32
  878.4 21.2 %reduce-scatter.21.cloned.1.call-done = bf16[320,60]{1,0:T(8,128)(2,1)} async-done(((bf16[2560,60]{1,0:T(8,128)(2,1)}), bf16[320,60]{1,0:T(8,128)(2,1)}) %reduce-scatter.21.cloned.1.call-update) | async-done | bytes 38416
  904.8 69.3 %all-reduce.7 = (f32[960]{0:T(1024)}, f32[960]{0:T(1024)}) all-reduce(f32[960]{0:T(1024)S(1)} %get-tuple-element.68, f32[960]{0:T(1024)S(1)} %get-tuple-element.66), channel_id=1, replica_groups=mesh['shard'=8,'ctx'=16] {'shard','ctx'}, use_global_device_ids=true, to_apply=%region_17.18 | all-reduce | flops 1920 | bytes 15360 | tf_op jit(solution)/shard_map/psum | solution.py:282
  (190 shorter events, 87.8 us)
Async XLA Ops:
  7.2 86.9 %all-gather.16.cloned.1.call-start = ((), (), s32[]{:S(2)}) async-start(), calls=%async_computation.8 | async-start | bytes 1566720 | tf_op jit(solution)/shard_map/all_gather | solution.py:19
  12.3 30.2 %copy-start.22 = (bf16[320,60]{0,1:T(8,128)(2,1)S(1)}, bf16[320,60]{0,1:T(8,128)(2,1)}, u32[]{:S(2)}) copy-start(bf16[320,60]{0,1:T(8,128)(2,1)} %param.20) | copy-start | bytes 115204
  39.4 27.0 %copy-start.25 = (s32[1,32]{1,0:T(1,128)S(1)}, s32[1,32]{1,0:T(1,128)}, u32[]{:S(2)}) copy-start(s32[1,32]{1,0:T(1,128)} %param.23) | copy-start | bytes 388
  39.4 32.3 %copy-start.1 = (bf16[256,960]{0,1:T(8,128)(2,1)S(1)}, bf16[256,960]{0,1:T(8,128)(2,1)}, u32[]{:S(2)}) copy-start(bf16[256,960]{0,1:T(8,128)(2,1)} %param.13) | copy-start | bytes 1474564
  40.5 103.0 %all-gather.20.cloned.1.call-start = ((), (), s32[]{:S(2)}) async-start(), calls=%async_computation.10 | async-start | bytes 2228224 | tf_op jit(solution)/shard_map/all_gather | solution.py:122
  41.5 151.4 %all-gather.18.cloned.1.call-start = ((), (), s32[]{:S(2)}) async-start(), calls=%async_computation.9 | async-start | bytes 2228224 | tf_op jit(solution)/shard_map/all_gather | solution.py:120
  42.4 212.0 %all-gather.22.cloned.1.call-start = ((), (), s32[]{:S(2)}) async-start(), calls=%async_computation.11 | async-start | bytes 5570560 | tf_op jit(solution)/shard_map/all_gather | solution.py:124
  65.1 30.4 %copy-start.23 = (f32[960]{0:T(1024)S(1)}, f32[960]{0:T(1024)}, u32[]{:S(2)}) copy-start(f32[960]{0:T(1024)} %param.21) | copy-start | bytes 11524
  66.4 253.7 %all-gather.12.cloned.1.call-start = ((), (), s32[]{:S(2)}) async-start(), calls=%async_computation.4 | async-start | bytes 5570560 | tf_op jit(solution)/shard_map/all_gather | solution.py:150
  97.4 302.2 %all-gather.14.cloned.1.call-start = ((), (), s32[]{:S(2)}) async-start(), calls=%async_computation.5 | async-start | bytes 10444800 | tf_op jit(solution)/shard_map/all_gather | solution.py:19
  99.5 485.5 %reduce-scatter.15.cloned.1.call-start = ((), (), s32[]{:S(2)}) async-start(), calls=%async_computation.6 | async-start | bytes 5570560 | tf_op jit(solution)/shard_map/reduce_scatter | solution.py:195
  197.4 64.4 %copy-start.5 = (bf16[256,960]{0,1:T(8,128)(2,1)S(1)}, bf16[256,960]{0,1:T(8,128)(2,1)}, u32[]{:S(2)}) copy-start(bf16[256,960]{0,1:T(8,128)(2,1)} %param.25) | copy-start | bytes 1474564
  324.6 25.2 %copy-start = (bf16[4096,320]{0,1:T(8,128)(2,1)}, bf16[4096,320]{0,1:T(8,128)(2,1)S(1)}, u32[]{:S(2)}) copy-start(bf16[4096,320]{0,1:T(8,128)(2,1)S(1)} %get-tuple-element.81) | copy-start | bytes 7864324
  349.8 26.3 %copy-start.3 = (bf16[960,960]{1,0:T(8,128)(2,1)S(1)}, bf16[960,960]{1,0:T(8,128)(2,1)}, u32[]{:S(2)}) copy-start(bf16[960,960]{1,0:T(8,128)(2,1)} %reshape.339) | copy-start | bytes 5529604
  399.6 5.7 copy-start.11
  399.6 12.3 %slice-start = ((s8[9830400]{0:T(1024)(128)(4,1)}), s8[4194304]{0:T(1024)(128)(4,1)S(1)}, s32[]{:S(2)}) async-start(s8[9830400]{0:T(1024)(128)(4,1)} %bitcast.173), calls=%async_computation.15 | async-start | bytes 8388608
  405.3 6.6 slice-start.1
  405.3 6.6 slice-start.2
  411.9 4.4 copy-start.15
  411.9 4.5 copy-start.14
  411.9 4.4 copy-start.10
  503.9 274.6 %all-reduce.11.cloned.1.call-start = ((), (), s32[]{:S(2)}) async-start(), calls=%async_computation.14 | async-start | bytes 2457600
  588.5 276.1 %reduce-scatter.19.cloned.1.call-start = ((), (), s32[]{:S(2)}) async-start(), calls=%async_computation.12 | async-start | bytes 10444800
  612.8 286.8 %reduce-scatter.21.cloned.1.call-start = ((), (), s32[]{:S(2)}) async-start(), calls=%async_computation.13 | async-start | bytes 737280
  633.7 127.3 %copy-start.26 = (u32[128]{0:T(128)S(1)}, u32[128]{0:T(128)}, u32[]{:S(2)}) copy-start(u32[128]{0:T(128)} %constant.141) | copy-start | bytes 1540
  755.1 9.9 collective-permute-start.2
  762.3 13.3 %collective-permute-start = (bf16[960,60]{0,1:T(8,128)(2,1)S(1)}, bf16[960,60]{0,1:T(8,128)(2,1)S(1)}, u32[]{:S(2)}, u32[]{:S(2)}) collective-permute-start(bf16[960,60]{0,1:T(8,128)(2,1)S(1)} %slice.72), channel_id=1, source_target_pairs={{0,1},{1,2},{2,3},{3,4},{4,5},{5,6},{6,7},{7,8},{8,9},{9,10},{10,1... | collective-permute-start | bytes 345608
  768.7 207.6 %reduce-scatter.17.cloned.1.call-start = ((), (), s32[]{:S(2)}) async-start(), calls=%async_computation.7 | async-start | bytes 1105920 | tf_op jit(solution)/shard_map/reduce_scatter | solution.py:30
  769.4 7.9 collective-permute-start.1
  873.3 27.9 %copy-start.8 = (bf16[320,1920]{1,0:T(8,128)(2,1)S(1)}, bf16[320,1920]{1,0:T(8,128)(2,1)}, u32[]{:S(2)}) copy-start(bf16[320,1920]{1,0:T(8,128)(2,1)} %copy-done.7) | copy-start | bytes 3686404
  873.3 27.9 %copy-start.17 = (bf16[256,5,64]{0,2,1:T(8,128)(2,1)S(1)}, bf16[256,5,64]{0,2,1:T(8,128)(2,1)}, u32[]{:S(2)}) copy-start(bf16[256,5,64]{0,2,1:T(8,128)(2,1)} %copy-done.16) | copy-start | bytes 491524
  878.4 24.5 %copy-start.21 = (bf16[256,640]{0,1:T(8,128)(2,1)S(1)}, bf16[256,640]{0,1:T(8,128)(2,1)}, u32[]{:S(2)}) copy-start(bf16[256,640]{0,1:T(8,128)(2,1)} %reduce-scatter.15.cloned.1.call-done) | copy-start | bytes 983044
  (12 other events, 24.9 us)
Sparse Core Ops, SparseCore 0:
  40.6 53.3 all-gather.15
  96.4 46.9 all-gather.19
  145.9 47.0 all-gather.17
  195.8 58.5 all-gather.21
  257.1 62.9 all-gather.11
  322.3 77.1 all-gather.13
  504.1 80.9 reduce-scatter.14
  588.6 163.1 all-reduce.10
  756.3 108.1 reduce-scatter.18
  866.9 32.5 reduce-scatter.20
  902.1 38.0 reduce-scatter.16
where the time goes:
time: 996 us; the launch traced here: 990 us
  waiting for transfers between devices  421 us (42%)
  blocking collectives  240 us (24%)
  matrix products  198 us (20%)
  local copies, waits for them, and re-layouts  69.4 us (7%)
  other arithmetic  26.9 us (3%)
  between operations  20 us (2%)
  starting transfers between devices  15.4 us (2%)
    unnamed x1, blocking collectives  121 us
    unnamed x17, waiting for transfers between devices  106 us
    reduce_scatter x1, waiting for transfers between devices, body(): lax.psum_scatter(block.astype(jnp.bfloat16), 'ctx', scatter_dimension=0,...  75.7 us
    psum x1, blocking collectives, body(): lax.psum((attention_gain_gradient, feedforward_gain_gradient), ('shard',...  69.3 us
    all_gather x1, waiting for transfers between devices, body(): lax.all_gather(row_part[6], 'ctx', axis=1, tiled=True)  57 us
    all_gather x1, waiting for transfers between devices, body(): lax.all_gather(kv_local, 'ctx', axis=0, tiled=True)  52.9 us
    unnamed x95, local copies, waits for them, and re-layouts  50.7 us
    all_gather x1, waiting for transfers between devices, body(): lax.all_gather(row_part[0], 'ctx', axis=1, tiled=True)  45.6 us
  transfers between devices with their start and end apart: 14, of which 11 were waited for; matrix products, arithmetic and copies ran while one was open for 30% of the time, Pallas kernels for 0%

commit v1 on v0

v1 whole, which is shorter than its diff:
```python
import jax
import jax.numpy as jnp
from jax import lax
from jax.experimental import pallas as pl
from jax.experimental.pallas import tpu as pltpu
from jax.sharding import Mesh
from jax.sharding import PartitionSpec as P

D = 960
HEADS = 15
KV_HEADS = 5
GROUP = 3
HEAD_DIM = 64
SPAN = 128
PAD = 1024

EPS = 1e-05
ROPE_BASE = 100000.0

BF = jnp.bfloat16
F32 = jnp.float32

PLANE = ("y", "x")
LINE = ("zh", "zl")
CHIPS = ("zl", "y", "x", "zh")
SEQ = ("x", "zh")
SWAP = [(0, 1), (1, 0)]


def pad_width(value):
    rows = value.shape[0]
    blocks = value.reshape(rows, 8, 120)
    return jnp.pad(blocks, ((0, 0), (0, 0), (0, 8))).reshape(rows, PAD)


def cut_width(value):
    rows = value.shape[0]
    return value.reshape(rows, 8, 128)[:, :, :120].reshape(rows, D)


def pad_lanes(value):
    return jnp.pad(value, ((0, 0), (0, 128 - value.shape[1])))


def other_core(value):
    return lax.ppermute(value, "c", SWAP)


def dot_last(left, right):
    return lax.dot_general(left, right, (((1,), (1,)), ((), ())), preferred_element_type=F32)


def dot_first(left, right):
    return lax.dot_general(left, right, (((0,), (0,)), ((), ())), preferred_element_type=F32)


def dot_plain(left, right):
    return jnp.dot(left, right, preferred_element_type=F32)


def key_rows_minus_query_lanes():
    row = lax.broadcasted_iota(jnp.int32, (SPAN, GROUP * SPAN), 0)
    lane = lax.broadcasted_iota(jnp.int32, (SPAN, GROUP * SPAN), 1)
    return row - lax.rem(lane, SPAN)


def second_tile(info, device):
    low = info[24 + device]
    mine = info[1]
    takes_low = low <= mine
    low_slot = info[8 + device]
    high_slot = 4 * device + 1 - low_slot
    slot = jnp.where(takes_low, low_slot, high_slot)
    half = jnp.where(takes_low, info[0], 1 - info[0])
    limit = jnp.where(low == mine, 0, SPAN)
    return slot, half, limit


def key_block(ref, slot):
    return ref[pl.ds(pl.multiple_of(slot * SPAN, SPAN), SPAN), :]


def attend_kernel(info, kv_ref, q_ref, out_ref, total_ref, query, numer, total):
    width = GROUP * SPAN
    query[...] = jnp.zeros_like(query)
    for half in range(2):
        query[half, :HEAD_DIM, :] = q_ref[0, half]
    numer[...] = jnp.zeros_like(numer)
    total[...] = jnp.zeros_like(total)
    diff = key_rows_minus_query_lanes()

    def add(half, keys, expo):
        numer[half] += dot_first(keys, expo.astype(BF))
        total[half] += jnp.sum(expo.reshape(expo.shape[0] // 8, 8, width), axis=0)

    def some(step, carry):
        high = 1 - info[0]
        keys = jnp.concatenate([key_block(kv_ref, info[8 + 4 * step + n]) for n in range(4)], axis=0)
        add(high, keys, jnp.exp(dot_plain(keys, query[high])))
        for n in range(4):
            slot, half, limit = second_tile(info, 4 * step + n)
            keys = key_block(kv_ref, slot)
            expo = jnp.exp(dot_plain(keys, query[half]))
            add(half, keys, jnp.where(diff <= limit, expo, 0.0))
        return carry

    lax.fori_loop(0, 4, some, 0)
    high = 1 - info[0]
    own = info[2]
    keys = key_block(kv_ref, 4 * own + 1 - info[8 + own])
    expo = jnp.exp(dot_plain(keys, query[high]))
    add(high, keys, jnp.where(diff <= 0, expo, 0.0))
    for half in range(2):
        summed = jnp.sum(total[half], axis=0, keepdims=True)
        total_ref[0, half] = summed
        out_ref[0, half] = numer[half, HEAD_DIM:, :] / summed


def attend(info, kv, query):
    width = GROUP * SPAN
    return pl.pallas_call(
        attend_kernel,
        grid_spec=pltpu.PrefetchScalarGridSpec(
            num_scalar_prefetch=1,
            grid=(KV_HEADS,),
            in_specs=[
                pl.BlockSpec((kv.shape[0], 2 * HEAD_DIM), lambda g, s: (0, g)),
                pl.BlockSpec((1, 2, HEAD_DIM, width), lambda g, s: (g, 0, 0, 0)),
            ],
            out_specs=[
                pl.BlockSpec((1, 2, HEAD_DIM, width), lambda g, s: (g, 0, 0, 0)),
                pl.BlockSpec((1, 2, 1, width), lambda g, s: (g, 0, 0, 0)),
            ],
            scratch_shapes=[
                pltpu.VMEM((2, 2 * HEAD_DIM, width), BF),
                pltpu.VMEM((2, 2 * HEAD_DIM, width), F32),
                pltpu.VMEM((2, 8, width), F32),
            ],
        ),
        out_shape=[
            jax.ShapeDtypeStruct((KV_HEADS, 2, HEAD_DIM, width), F32),
            jax.ShapeDtypeStruct((KV_HEADS, 2, 1, width), F32),
        ],
        compiler_params=pltpu.CompilerParams(vmem_limit_bytes=48 * 1024 * 1024),
        cost_estimate=pl.CostEstimate(flops=4 * 10**9, bytes_accessed=8 * 10**6, transcendentals=8 * 10**6),
    )(info, kv, query)


def attend_back_kernel(info, kv_ref, q_ref, dnum_ref, delta_ref, dq_ref, dkv_ref, wide, tall, dq, dkv):
    width = GROUP * SPAN
    for half in range(2):
        zero = jnp.zeros((HEAD_DIM, width), BF)
        both = jnp.concatenate(
            [
                jnp.concatenate([q_ref[0, half], zero], axis=1),
                jnp.concatenate([zero, dnum_ref[0, half]], axis=1),
            ],
            axis=0,
        )
        wide[half] = both
        tall[half] = both.T
    dq[...] = jnp.zeros_like(dq)
    dkv[...] = jnp.zeros_like(dkv)
    diff = key_rows_minus_query_lanes()

    def tile(half, slot, limit):
        keys = key_block(kv_ref, slot)
        scores = dot_plain(keys, wide[half])
        expo = jnp.exp(scores[:, :width])
        if limit is not None:
            expo = jnp.where(diff <= limit, expo, 0.0)
        grads = (expo * (scores[:, width:] - delta_ref[0, half])).astype(BF)
        pair = jnp.concatenate([grads, expo.astype(BF)], axis=1)
        at = pl.ds(pl.multiple_of(slot * SPAN, SPAN), SPAN)
        dkv[at, :] += dot_plain(pair, tall[half])
        dq[half] += dot_first(keys, grads)

    def some(step, carry):
        for n in range(2):
            device = 2 * step + n
            tile(1 - info[0], info[8 + device], None)
            slot, half, limit = second_tile(info, device)
            tile(half, slot, limit)
        return carry

    lax.fori_loop(0, 8, some, 0)
    own = info[2]
    tile(1 - info[0], 4 * own + 1 - info[8 + own], 0)
    for half in range(2):
        dq_ref[0, half] = dq[half, :HEAD_DIM, :] * (HEAD_DIM**-0.5)
    dkv_ref[...] = dkv[...].astype(BF)


def attend_back(info, kv, query, dnum, delta):
    width = GROUP * SPAN
    rows = kv.shape[0]
    head = pl.BlockSpec((1, 2, HEAD_DIM, width), lambda g, s: (g, 0, 0, 0))
    return pl.pallas_call(
        attend_back_kernel,
        grid_spec=pltpu.PrefetchScalarGridSpec(
            num_scalar_prefetch=1,
            grid=(KV_HEADS,),
            in_specs=[
                pl.BlockSpec((rows, 2 * HEAD_DIM), lambda g, s: (0, g)),
                head,
                head,
                pl.BlockSpec((1, 2, 1, width), lambda g, s: (g, 0, 0, 0)),
            ],
            out_specs=[head, pl.BlockSpec((rows, 2 * HEAD_DIM), lambda g, s: (0, g))],
            scratch_shapes=[
                pltpu.VMEM((2, 2 * HEAD_DIM, 2 * width), BF),
                pltpu.VMEM((2, 2 * width, 2 * HEAD_DIM), BF),
                pltpu.VMEM((2, 2 * HEAD_DIM, width), F32),
                pltpu.VMEM((rows, 2 * HEAD_DIM), F32),
            ],
        ),
        out_shape=[
            jax.ShapeDtypeStruct((KV_HEADS, 2, HEAD_DIM, width), F32),
            jax.ShapeDtypeStruct((rows, KV_HEADS * 2 * HEAD_DIM), BF),
        ],
        compiler_params=pltpu.CompilerParams(vmem_limit_bytes=48 * 1024 * 1024),
        cost_estimate=pl.CostEstimate(flops=10 * 10**9, bytes_accessed=12 * 10**6, transcendentals=8 * 10**6),
    )(info, kv, query, dnum, delta)


def by_half(value):
    split = value.reshape(KV_HEADS, GROUP, HEAD_DIM, 2, SPAN)
    return split.transpose(0, 3, 2, 1, 4).reshape(KV_HEADS, 2, HEAD_DIM, GROUP * SPAN)


def by_head(value):
    rows = value.shape[2]
    split = value.reshape(KV_HEADS, 2, rows, GROUP, SPAN)
    return split.transpose(0, 3, 2, 1, 4).reshape(HEADS, rows, 2 * SPAN)


def rotate(value, cosine, sine):
    first, second = value[:, :32], value[:, 32:]
    return jnp.concatenate([first * cosine - second * sine, second * cosine + first * sine], axis=1)


def unrotate(value, cosine, sine):
    first, second = value[:, :32], value[:, 32:]
    return jnp.concatenate([first * cosine + second * sine, second * cosine - first * sine], axis=1)


def norm_forward(value, gain):
    inverse = lax.rsqrt(jnp.sum(value * value, axis=-1, keepdims=True) / D + EPS)
    unit = value * inverse
    return unit, inverse, (unit * gain).astype(BF)


def norm_back(grad, unit, inverse, gain):
    scaled = grad * gain
    inner = jnp.sum(scaled * unit, axis=-1, keepdims=True) / D
    return inverse * (scaled - unit * inner), jnp.sum(grad * unit, axis=0)


def body(
    tokens,
    w_query,
    w_key,
    w_value,
    w_out,
    w_gate,
    w_up,
    w_down,
    attention_norm_gain,
    feedforward_norm_gain,
    span_order,
    positions,
    out_grad,
):
    rows = tokens.shape[0]
    core = lax.axis_index("c")
    me = lax.axis_index(("x", "zh", "c"))

    mixed = jnp.concatenate([w_down.reshape(2, 160, 60), w_out.reshape(2, 60, 60)], axis=1)
    mixed = lax.all_to_all(mixed, "c", 0, 0, tiled=True)
    mixed = jnp.concatenate([mixed[0], mixed[1]], axis=1)
    big = jnp.concatenate([w_gate.T, w_up.T, mixed], axis=0)
    big = jnp.pad(pad_lanes(big), ((0, 4), (0, 0)))
    big = lax.all_gather(big, LINE, axis=0, tiled=True)
    big = lax.all_gather(big, PLANE, axis=0, tiled=True).reshape(4, 4, 2, 2, 544, 128)

    small = pad_lanes(jnp.concatenate([w_query.T, w_key.T, w_value.T], axis=0))
    small = lax.all_to_all(jnp.broadcast_to(small, (64, 100, 128)), CHIPS, 0, 0, tiled=True)
    small = lax.all_to_all(jnp.broadcast_to(small, (2, 64, 100, 128)), "c", 0, 0, tiled=True)
    small = small.reshape(2, 2, 4, 4, 2, 100, 128).transpose(3, 4, 0, 5, 1, 2, 6)
    w_q = small[:, :, :, :60].reshape(D, PAD)
    w_k = small[:, :, :, 60:80].reshape(KV_HEADS, HEAD_DIM, PAD)
    w_v = small[:, :, :, 80:].reshape(KV_HEADS, HEAD_DIM, PAD)
    w_kv = jnp.concatenate([w_k, w_v], axis=1).reshape(2 * KV_HEADS * HEAD_DIM, PAD)
    w_qkv = jnp.concatenate([w_q, w_kv], axis=0)

    order = span_order[0]
    pairs = order.reshape(16, 2)
    low_half = (pairs[:, 0] > pairs[:, 1]).astype(jnp.int32)
    low_span = jnp.minimum(pairs[:, 0], pairs[:, 1])
    own_pair = lax.dynamic_slice_in_dim(order, 2 * me, 2)
    own_low_half = (own_pair[0] > own_pair[1]).astype(jnp.int32)
    head_info = jnp.stack([own_low_half, jnp.minimum(own_pair[0], own_pair[1]), me.astype(jnp.int32)])
    info = jnp.concatenate(
        [
            head_info,
            jnp.zeros((5,), jnp.int32),
            2 * jnp.arange(16, dtype=jnp.int32) + low_half,
            low_span,
        ]
    ).astype(jnp.int32)
    place = jnp.concatenate(
        [
            lax.dynamic_slice_in_dim(positions[0], own_pair[0] * SPAN, SPAN, 0),
            lax.dynamic_slice_in_dim(positions[0], own_pair[1] * SPAN, SPAN, 0),
        ]
    )
    half_dim = HEAD_DIM // 2
    freq = jnp.power(ROPE_BASE, -jnp.arange(half_dim, dtype=F32) / half_dim)
    angle = freq[:, None] * place.astype(F32)[None, :]
    cosine, sine = jnp.cos(angle), jnp.sin(angle)

    gain_one = pad_width(attention_norm_gain[None])
    gain_two = pad_width(feedforward_norm_gain[None])
    layer_input = pad_width(tokens).astype(F32)
    dy = pad_width(out_grad)
    dy_both = jnp.concatenate([dy, other_core(dy)], axis=0)

    unit_one, inverse_one, normed_one = norm_forward(layer_input, gain_one)
    qkv = dot_last(w_qkv, normed_one)
    query = rotate(qkv[:D].reshape(HEADS, HEAD_DIM, rows), cosine, sine).astype(BF)
    key_value = qkv[D:].reshape(KV_HEADS, 2, HEAD_DIM, rows)
    key = rotate(key_value[:, 0], cosine, sine).astype(BF)
    kv_local = jnp.stack([key, key_value[:, 1].astype(BF)], axis=1)
    kv_local = kv_local.reshape(2 * KV_HEADS * HEAD_DIM, rows).T
    query = by_half(query.reshape(D, rows) * BF(HEAD_DIM**-0.5))

    kv = lax.all_to_all(jnp.broadcast_to(kv_local, (8, rows, 640)), SEQ, 0, 0, tiled=True)
    kv = lax.all_to_all(jnp.broadcast_to(kv, (2, 8, rows, 640)), "c", 0, 0, tiled=True)
    kv = kv.transpose(1, 0, 2, 3).reshape(16 * rows, 640)

    attended, total = attend(info, kv, query)
    attended = by_head(attended)
    total = by_head(total)
    attended_low = attended.astype(BF).reshape(D, rows)

    w_gate_t = big[:, :, :, :, :160].transpose(1, 2, 4, 3, 0, 5).reshape(1280, PAD)
    w_up_t = big[:, :, :, :, 160:320].transpose(1, 2, 4, 3, 0, 5).reshape(1280, PAD)
    w_down_h = big[:, :, :, :, 320:480].transpose(3, 0, 4, 1, 2, 5).reshape(1280, PAD)
    w_out_h = big[:, :, :, :, 480:540].transpose(3, 0, 4, 1, 2, 5).reshape(8, 60, PAD)
    w_out_o = other_core(w_out_h)
    first = core == 0
    w_out_full = jnp.stack(
        [jnp.where(first, w_out_h, w_out_o), jnp.where(first, w_out_o, w_out_h)], axis=1
    ).reshape(D, PAD)

    hidden = layer_input + dot_first(attended_low, w_out_full)
    unit_two, inverse_two, normed_two = norm_forward(hidden, gain_two)
    normed_both = jnp.concatenate([normed_two, other_core(normed_two)], axis=0)
    gate = dot_last(normed_both, w_gate_t)
    upward = dot_last(normed_both, w_up_t)
    sigma = jax.nn.sigmoid(gate)
    silu_gate = gate * sigma
    active = (silu_gate * upward).astype(BF)
    dact = dot_last(dy_both, w_down_h)
    dgate = (dact * upward * sigma * (1.0 + gate * (1.0 - sigma))).astype(BF)
    dup = (dact * silu_gate).astype(BF)
    dn_two = dot_plain(dgate, w_gate_t) + dot_plain(dup, w_up_t)
    dn_two = dn_two[:rows] + other_core(dn_two[rows:].astype(BF)).astype(F32)
    fed = dot_plain(active, w_down_h)
    fed = fed[:rows] + other_core(fed[rows:].astype(BF)).astype(F32)
    result = cut_width((hidden + fed).astype(BF))

    back_two, gain_two_grad = norm_back(dn_two, unit_two, inverse_two, gain_two)
    dh = dy.astype(F32) + back_two
    dh_low = dh.astype(BF)
    dob = dot_last(w_out_full, dh_low).astype(BF).reshape(HEADS, HEAD_DIM, rows)
    dob = dob.astype(F32)
    dnum = (dob / total).astype(BF)
    delta = jnp.sum(dob * attended, axis=1, keepdims=True) / total
    delta = delta.reshape(KV_HEADS, GROUP, 1, 2, SPAN).transpose(0, 3, 2, 1, 4)
    delta = delta.reshape(KV_HEADS, 2, 1, GROUP * SPAN)

    g_gate = dot_first(dgate, normed_both).astype(BF).reshape(4, 2, 160, 2, 4, 128)
    g_up = dot_first(dup, normed_both).astype(BF).reshape(4, 2, 160, 2, 4, 128)
    g_down = dot_first(active, dy_both).astype(BF).reshape(2, 4, 160, 4, 2, 128)
    g_out = dot_plain(attended_low, dh_low).astype(BF).reshape(8, 2, 60, PAD)
    keep = lax.dynamic_index_in_dim(g_out, core, 1, keepdims=False)
    give = lax.dynamic_index_in_dim(g_out, 1 - core, 1, keepdims=False)
    g_out = (keep.astype(F32) + other_core(give).astype(F32)).astype(BF).reshape(2, 4, 60, 4, 2, 128)
    g_big = jnp.concatenate(
        [
            g_gate.transpose(4, 0, 1, 3, 2, 5),
            g_up.transpose(4, 0, 1, 3, 2, 5),
            g_down.transpose(1, 3, 4, 0, 2, 5),
            g_out.transpose(1, 3, 4, 0, 2, 5),
            jnp.zeros((4, 4, 2, 2, 4, 128), BF),
        ],
        axis=4,
    ).reshape(64 * 544, 128)
    g_big = lax.psum_scatter(g_big, PLANE, scatter_dimension=0, tiled=True)
    g_big = lax.psum_scatter(g_big, LINE, scatter_dimension=0, tiled=True)

    dq, dkv = attend_back(info, kv, query, by_half(dnum.reshape(D, rows)), delta)

    dkv = dkv.reshape(8, 2, rows, 640)
    keep = lax.dynamic_index_in_dim(dkv, core, 1, keepdims=False)
    give = lax.dynamic_index_in_dim(dkv, 1 - core, 1, keepdims=False)
    dkv = (keep.astype(F32) + other_core(give).astype(F32)).astype(BF)
    dkv = lax.all_to_all(dkv, SEQ, 0, 0, tiled=True)
    dkv = jnp.sum(dkv.astype(F32), axis=0).T.reshape(KV_HEADS, 2, HEAD_DIM, rows)

    dq_low = unrotate(by_head(dq), cosine, sine).astype(BF).reshape(D, rows)
    dk_low = unrotate(dkv[:, 0], cosine, sine).astype(BF)
    dkv_low = jnp.stack([dk_low, dkv[:, 1].astype(BF)], axis=1).reshape(640, rows)
    dqkv = jnp.concatenate([dq_low, dkv_low], axis=0)
    dn_one = dot_first(dqkv, w_qkv)
    back_one, gain_one_grad = norm_back(dn_one, unit_one, inverse_one, gain_one)
    input_grad = cut_width((dh + back_one).astype(BF))

    g_qkv = dot_plain(dqkv, normed_one).astype(BF)
    g_q = g_qkv[:D].reshape(8, 2, 60, PAD)
    g_kv = g_qkv[D:].reshape(KV_HEADS, 2, HEAD_DIM, PAD)
    g_k = g_kv[:, 0].reshape(8, 2, 20, PAD)
    g_v = g_kv[:, 1].reshape(8, 2, 20, PAD)
    g_small = jnp.concatenate([g_q, g_k, g_v], axis=2)
    keep = lax.dynamic_index_in_dim(g_small, core, 1, keepdims=False)
    give = lax.dynamic_index_in_dim(g_small, 1 - core, 1, keepdims=False)
    g_small = (keep.astype(F32) + other_core(give).astype(F32)).astype(BF)
    g_small = g_small.reshape(8, 100, 8, 128).transpose(2, 0, 1, 3).reshape(64, 100, 128)
    gains = jnp.stack([gain_one_grad, gain_two_grad])
    gains = gains + other_core(gains)
    gains_high = gains.astype(BF)
    gains_low = (gains - gains_high.astype(F32)).astype(BF)
    gains = jnp.concatenate([gains_high.reshape(16, 128), gains_low.reshape(16, 128)], axis=0)
    last = jnp.concatenate([g_small, jnp.broadcast_to(gains, (64, 32, 128))], axis=1)
    last = lax.all_to_all(last, CHIPS, 0, 0, tiled=True)
    last = jnp.sum(last.astype(F32), axis=0)
    gains = cut_width((last[100:116] + last[116:132]).reshape(2, PAD))

    g_big = g_big.astype(F32)
    mixed = g_big[320:540, :120].reshape(220, 2, 60).transpose(1, 0, 2)
    mixed = lax.all_to_all(mixed, "c", 0, 0, tiled=True)
    return (
        result,
        input_grad,
        last[:60, :120].T,
        last[60:80, :120].T,
        last[80:100, :120].T,
        mixed[:, 160:].reshape(120, 60),
        g_big[:160, :120].T,
        g_big[160:320, :120].T,
        mixed[:, :160].reshape(320, 60),
        gains[0],
        gains[1],
    )


def solution(mesh):
    fine = Mesh(mesh.devices.reshape(2, 4, 4, 2, 2), ("zl", "y", "x", "zh", "c"))
    shard, ctx = ("zl", "y"), ("x", "zh", "c")
    both = shard + ctx
    return jax.shard_map(
        body,
        mesh=fine,
        in_specs=(P(both, None),)
        + (P(shard, ctx),) * 7
        + (P(), P(), P(shard, None), P(shard, None), P(both, None)),
        out_specs=(P(both, None), P(both, None)) + (P(shard, ctx),) * 7 + (P(), P()),
        check_vma=False,
    )
```

time: 996 us -> 551 us (0.55)
  waiting for transfers between devices: 421 us -> 103 us
  blocking collectives: 240 us -> 40.3 us
  matrix products: 198 us -> 40.6 us
  local copies, waits for them, and re-layouts: 69.4 us -> 193 us
  Pallas kernels: 0 us -> 81.7 us
  starting transfers between devices: 15.4 us -> 40.9 us
    all_gather x6 -> x1, waiting for transfers between devices: 239 us -> 0.01 us  [body(): lax.all_gather(big, PLANE, axis=0, tiled=True).reshape(4, 4, 2, 2, 544, 128)]
    dot_general x27 -> x15, matrix products: 198 us -> 40.6 us  [the longest x5 18.1 us: dot_first(): lax.dot_general(left, right, (((0,), (0,)), ((), ())), preferred_element_...]
    unnamed x1 -> x0, blocking collectives: 121 us -> none
    unnamed x17 -> x3, waiting for transfers between devices: 106 us -> 0.05 us
    all_to_all x0 -> x5, waiting for transfers between devices: none -> 95.3 us  [the longest x1 34.5 us: body(): dkv = lax.all_to_all(dkv, SEQ, 0, 0, tiled=True)]
    pallas_call x0 -> x2, Pallas kernels: none -> 81.7 us  [the longest x1 54 us: attend_back(): pl.pallas_call(attend_back_kernel, grid_spec=pltpu.PrefetchScalarGridSpec...]
    reduce_scatter x2, waiting for transfers between devices: 75.7 us -> 1.89 us  [the longest x1 1.89 us: body(): g_big = lax.psum_scatter(g_big, LINE, scatter_dimension=0, tiled=True)]
    psum x1 -> x0, blocking collectives: 69.3 us -> none  [body(): lax.psum((attention_gain_gradient, feedforward_gain_gradient), ('shard',...]
  transfers between devices with their start and end apart: 14 -> 17, of which waited for: 11 -> 7; matrix products, arithmetic and copies ran while one was open for 30% -> 35% of each run, Pallas kernels for 0% -> 15%
where the time goes in v1:
time: 551 us; the launch traced here: 544 us
  local copies, waits for them, and re-layouts  193 us (35%)
  waiting for transfers between devices  103 us (19%)
  Pallas kernels  81.7 us (15%)
  starting transfers between devices  40.9 us (7%)
  matrix products  40.6 us (7%)
  blocking collectives  40.3 us (7%)
  other arithmetic  26.3 us (5%)
  between operations  19 us (3%)
    pallas_call x1, Pallas kernels, attend_back(): pl.pallas_call(attend_back_kernel, grid_spec=pltpu.PrefetchScalarGridSpec...  54 us
    all_to_all x1, waiting for transfers between devices, body(): dkv = lax.all_to_all(dkv, SEQ, 0, 0, tiled=True)  34.5 us
    unnamed x96, local copies, waits for them, and re-layouts  31.3 us
    pallas_call x1, Pallas kernels, attend(): pl.pallas_call(attend_kernel, grid_spec=pltpu.PrefetchScalarGridSpec(num_...  27.8 us
    all_to_all x1, waiting for transfers between devices, body(): last = lax.all_to_all(last, CHIPS, 0, 0, tiled=True)  25 us
    all_to_all x1, waiting for transfers between devices, body(): lax.all_to_all(jnp.broadcast_to(small, (64, 100, 128)), CHIPS, 0, 0, tile...  23.2 us
    dot_general x5, matrix products, dot_first(): lax.dot_general(left, right, (((0,), (0,)), ((), ())), preferred_element_...  18.1 us
    dot_general x5, matrix products, dot_last(): lax.dot_general(left, right, (((1,), (1,)), ((), ())), preferred_element_...  14.6 us
  transfers between devices with their start and end apart: 17, of which 7 were waited for; matrix products, arithmetic and copies ran while one was open for 35% of the time, Pallas kernels for 15%

profile of v1, /device:TPU:1, one launch (start us, length us, event | category | flops | bytes accessed | tf_op | source)
XLA Modules:
  0.0 544.1 jit_solution(9783528301135441900)
XLA Ops:
  9.7 4.7 all-to-all-start.4
  16.5 12.9 %all_gather.6 = bf16[2176,128]{1,0:T(8,128)(2,1)} all-gather(bf16[544,128]{1,0:T(8,128)(2,1)S(1)} %pad.74), channel_id=1, replica_groups=mesh['zl'=2,'y'=4,'x'=4,'zh'=2,'c'=2] {'zh','zl'}, dimensions={0}, use_global_device_ids=true | all-gather | bytes 696320 | tf_op jit(solution)/shard_map/all_gather | solution.py:283
  30.9 9.7 %all-to-all-start = ((bf16[64,100,128]{2,1,0:T(8,128)(2,1)}), bf16[64,100,128]{2,1,0:T(8,128)(2,1)S(1)}, u32[]{:S(2)}, u32[]{:S(2)}) async-start(bf16[64,100,128]{2,1,0:T(8,128)(2,1)} %broadcast_in_dim.12), calls=%async_computation | async-start | bytes 3407872 | tf_op jit(solution)/shard_map/all_to_all | solution.py:287
  45.1 23.2 %all-to-all-done = bf16[64,100,128]{2,1,0:T(8,128)(2,1)S(1)} async-done(((bf16[64,100,128]{2,1,0:T(8,128)(2,1)}), bf16[64,100,128]{2,1,0:T(8,128)(2,1)S(1)}, u32[]{:S(2)}, u32[]{:S(2)}) %all-to-all-start) | async-done | bytes 1638432 | tf_op jit(solution)/shard_map/all_to_all | solution.py:287
  69.6 13.5 %all_to_all.40 = bf16[2,64,100,128]{3,1,2,0:T(8,128)(2,1)S(1)} all-to-all(bf16[2,64,100,128]{3,1,2,0:T(8,128)(2,1)S(1)} %broadcast_in_dim.13), channel_id=1, replica_groups=mesh['zl'=2,'y'=4,'x'=4,'zh'=2,'c'=2] {'c'}, dimensions={0} | all-to-all | bytes 6553600 | tf_op jit(solution)/shard_map/all_to_all | solution.py:288
  96.7 4.4 reshape.403
  107.6 3.8 all-to-all-start.2
  137.8 12.7 %all-to-all-done.2 = bf16[8,256,640]{2,1,0:T(8,128)(2,1)S(1)} async-done(((bf16[8,256,640]{2,1,0:T(8,128)(2,1)}), bf16[8,256,640]{2,1,0:T(8,128)(2,1)S(1)}, u32[]{:S(2)}, u32[]{:S(2)}) %all-to-all-start.2) | async-done | bytes 2621472 | tf_op jit(solution)/shard_map/all_to_all | solution.py:337
  151.2 8.4 %all_to_all.41 = bf16[2,8,256,640]{3,2,1,0:T(8,128)(2,1)S(1)} all-to-all(bf16[2,8,256,640]{3,2,1,0:T(8,128)(2,1)S(1)} %broadcast_in_dim.15), channel_id=1, replica_groups=mesh['zl'=2,'y'=4,'x'=4,'zh'=2,'c'=2] {'c'}, dimensions={0} | all-to-all | bytes 10485760 | tf_op jit(solution)/shard_map/all_to_all | solution.py:338
  162.4 27.8 %shard_map.212 = (f32[5,2,64,384]{3,2,1,0:T(8,128)S(1)}, f32[5,2,1,384]{3,2,1,0:T(1,128)S(1)}) custom-call(s32[40]{0:T(128)S(1)} %concatenate.91.info, bf16[4096,640]{1,0:T(8,128)(2,1)} %bitcast.272, bf16[5,2,64,384]{3,2,1,0:T(8,128)(2,1)S(1)} %reshape.411.q_ref), custom_call_target="tpu_custom_call" | custom-call | flops 4000000000 | bytes 8000000 | tf_op jit(solution)/shard_map/pallas_call | solution.py:121
  205.0 5.3 slice_bitcast_fusion
  213.8 5.4 %reshape.418 = bf16[1280,1024]{1,0:T(8,128)(2,1)} reshape(bf16[4,2,160,2,4,128]{5,4,3,2,1,0:T(4,128)(2,1)} %copy.348) | data formatting | bytes 5242880 | tf_op jit(solution)/shard_map/reshape | solution.py:346
  219.2 5.3 copy.349
  224.5 5.4 %reshape.419 = bf16[1280,1024]{1,0:T(8,128)(2,1)} reshape(bf16[4,2,160,2,4,128]{5,4,3,2,1,0:T(4,128)(2,1)} %copy.349) | data formatting | bytes 5242880 | tf_op jit(solution)/shard_map/reshape | solution.py:347
  229.9 6.0 %copy.350 = bf16[2,4,160,4,2,128]{5,4,3,2,1,0:T(2,128)(2,1)} copy(bf16[2,4,160,4,2,128]{5,2,0,4,3,1:T(8,128)(2,1)} %get-tuple-element.25) | data formatting | bytes 5242880 | tf_op jit(solution)/shard_map/transpose | solution.py:348
  235.9 5.6 %reshape.420 = bf16[1280,1024]{1,0:T(8,128)(2,1)} reshape(bf16[2,4,160,4,2,128]{5,4,3,2,1,0:T(2,128)(2,1)} %copy.350) | data formatting | bytes 5242880 | tf_op jit(solution)/shard_map/reshape | solution.py:348
  248.3 3.8 multiply_convert_fusion
  253.7 5.1 convolution_convert_fusion
  265.8 4.3 convolution_convert_fusion.2
  270.1 4.3 convolution_convert_fusion.1
  274.3 5.5 %reshape.441 = bf16[4,2,160,2,4,128]{5,4,3,2,1,0:T(4,128)(2,1)} reshape(bf16[1280,1024]{1,0:T(8,128)(2,1)} %convolution_convert_fusion.2) | data formatting | bytes 5242880 | tf_op jit(solution)/shard_map/reshape | solution.py:383
  279.8 5.5 %reshape.442 = bf16[4,2,160,2,4,128]{5,4,3,2,1,0:T(4,128)(2,1)} reshape(bf16[1280,1024]{1,0:T(8,128)(2,1)} %convolution_convert_fusion.1) | data formatting | bytes 5242880 | tf_op jit(solution)/shard_map/reshape | solution.py:384
  285.3 5.4 %reshape.443 = bf16[2,4,160,4,2,128]{5,4,3,2,1,0:T(2,128)(2,1)} reshape(bf16[1280,1024]{1,0:T(8,128)(2,1)} %convolution_convert_fusion) | data formatting | bytes 5242880 | tf_op jit(solution)/shard_map/reshape | solution.py:385
  315.8 4.1 reshape.445
  323.2 9.1 %copy.375 = bf16[4,4,2,2,544,128]{5,4,3,2,1,0:T(8,128)(2,1)} copy(bf16[4,4,2,2,544,128]{5,0,3,4,2,1:T(4,128)(2,1)} %broadcast_dynamic-update-slice_fusion) | data formatting | bytes 17825792 | tf_op jit(solution)/shard_map/concatenate | solution.py:390
  340.3 54.0 %shard_map.213 = (f32[5,2,64,384]{3,2,1,0:T(8,128)S(1)}, bf16[4096,640]{1,0:T(8,128)(2,1)}) custom-call(s32[40]{0:T(128)S(1)} %concatenate.91.info, bf16[4096,640]{1,0:T(8,128)(2,1)} %bitcast.273, bf16[5,2,64,384]{3,2,1,0:T(8,128)(2,1)S(1)} %reshape.411.q_ref, bf16[5,2,64,384]{3,2,1,0:T(8,128)(2,1)S(1)} %reshape.426.dnum_ref, ...), custom_call_target="tpu_custom_call" | custom-call | flops 10000000000 | bytes 12000000 | tf_op jit(solution)/shard_map/pallas_call | solution.py:198
  396.9 4.5 collective-permute-done.5
  403.7 7.0 %all-to-all-start.5 = ((bf16[8,256,640]{2,1,0:T(8,128)(2,1)}), bf16[8,256,640]{2,1,0:T(8,128)(2,1)}, u32[]{:S(2)}, u32[]{:S(2)}) async-start(bf16[8,256,640]{2,1,0:T(8,128)(2,1)} %fusion), calls=%async_computation.5 | async-start | bytes 5242880 | tf_op jit(solution)/shard_map/all_to_all | solution.py:409
  415.0 34.5 %all-to-all-done.5 = bf16[8,256,640]{2,1,0:T(8,128)(2,1)} async-done(((bf16[8,256,640]{2,1,0:T(8,128)(2,1)}), bf16[8,256,640]{2,1,0:T(8,128)(2,1)}, u32[]{:S(2)}, u32[]{:S(2)}) %all-to-all-start.5) | async-done | bytes 2621472 | tf_op jit(solution)/shard_map/all_to_all | solution.py:409
  480.6 11.2 %all-to-all-start.6 = ((bf16[64,132,128]{2,1,0:T(8,128)(2,1)}), bf16[64,132,128]{2,1,0:T(8,128)(2,1)}, u32[]{:S(2)}, u32[]{:S(2)}) async-start(bf16[64,132,128]{2,1,0:T(8,128)(2,1)} %copy.370), calls=%async_computation.6 | async-start | bytes 4456448 | tf_op jit(solution)/shard_map/all_to_all | solution.py:436
  496.0 25.0 %all-to-all-done.6 = bf16[64,132,128]{2,1,0:T(8,128)(2,1)} async-done(((bf16[64,132,128]{2,1,0:T(8,128)(2,1)}), bf16[64,132,128]{2,1,0:T(8,128)(2,1)}, u32[]{:S(2)}, u32[]{:S(2)}) %all-to-all-start.6) | async-done | bytes 2162720 | tf_op jit(solution)/shard_map/all_to_all | solution.py:436
  528.4 5.6 %all_to_all.42 = f32[2,220,60]{1,2,0:T(8,128)S(1)} all-to-all(f32[2,220,60]{1,2,0:T(8,128)S(1)} %bitcast.299), channel_id=1, replica_groups=mesh['zl'=2,'y'=4,'x'=4,'zh'=2,'c'=2] {'c'}, dimensions={0} | all-to-all | bytes 211200 | tf_op jit(solution)/shard_map/all_to_all | solution.py:442
  (273 shorter events, 182.2 us)
Async XLA Ops:
  7.2 22.2 %copy-start.35 = (bf16[120,20]{0,1:T(8,128)(2,1)S(1)}, bf16[120,20]{0,1:T(8,128)(2,1)}, u32[]{:S(2)}) copy-start(bf16[120,20]{0,1:T(8,128)(2,1)} %param.16) | copy-start | bytes 14404
  7.2 22.2 %copy-start.36 = (bf16[120,20]{0,1:T(8,128)(2,1)S(1)}, bf16[120,20]{0,1:T(8,128)(2,1)}, u32[]{:S(2)}) copy-start(bf16[120,20]{0,1:T(8,128)(2,1)} %param.15) | copy-start | bytes 14404
  7.2 22.2 %copy-start.34 = (bf16[120,60]{0,1:T(8,128)(2,1)S(1)}, bf16[120,60]{0,1:T(8,128)(2,1)}, u32[]{:S(2)}) copy-start(bf16[120,60]{0,1:T(8,128)(2,1)} %param.14) | copy-start | bytes 43204
  9.7 6.5 %all-to-all-start.4 = ((bf16[2,220,60]{1,2,0:T(8,128)(2,1)}), bf16[2,220,60]{1,2,0:T(8,128)(2,1)S(1)}, u32[]{:S(2)}, u32[]{:S(2)}) async-start(bf16[2,220,60]{1,2,0:T(8,128)(2,1)} %copy.344), calls=%async_computation.4 | async-start | bytes 131072 | tf_op jit(solution)/shard_map/all_to_all | solution.py:279
  14.4 110.4 %all-gather.2.cloned.1.call-start = ((), (), s32[]{:S(2)}) async-start(), calls=%async_computation.10 | async-start | bytes 9469952 | tf_op jit(solution)/shard_map/all_gather | solution.py:284
  29.4 11.2 %copy-start.39 = (s32[1,32]{1,0:T(1,128)S(1)}, s32[1,32]{1,0:T(1,128)}, u32[]{:S(2)}) copy-start(s32[1,32]{1,0:T(1,128)} %param.23) | copy-start | bytes 388
  29.4 13.2 %copy-start.32 = (bf16[256,960]{0,1:T(8,128)(2,1)S(1)}, bf16[256,960]{0,1:T(8,128)(2,1)}, u32[]{:S(2)}) copy-start(bf16[256,960]{0,1:T(8,128)(2,1)} %param.13) | copy-start | bytes 1474564
  30.9 12.1 %copy-start.37 = (f32[960]{0:T(1024)S(1)}, f32[960]{0:T(1024)}, u32[]{:S(2)}) copy-start(f32[960]{0:T(1024)} %param.21) | copy-start | bytes 11524
  30.9 37.4 %all-to-all-start = ((bf16[64,100,128]{2,1,0:T(8,128)(2,1)}), bf16[64,100,128]{2,1,0:T(8,128)(2,1)S(1)}, u32[]{:S(2)}, u32[]{:S(2)}) async-start(bf16[64,100,128]{2,1,0:T(8,128)(2,1)} %broadcast_in_dim.12), calls=%async_computation | async-start | bytes 3407872 | tf_op jit(solution)/shard_map/all_to_all | solution.py:287
  44.9 56.4 %copy-start.4 = (f32[256,8,128]{2,1,0:T(8,128)}, f32[256,8,128]{2,1,0:T(8,128)S(1)}, u32[]{:S(2)}) copy-start(f32[256,8,128]{2,1,0:T(8,128)S(1)} %pad_convert_fusion) | copy-start | bytes 3145732
  96.7 4.4 copy-start.17
  107.6 42.9 %all-to-all-start.2 = ((bf16[8,256,640]{2,1,0:T(8,128)(2,1)}), bf16[8,256,640]{2,1,0:T(8,128)(2,1)S(1)}, u32[]{:S(2)}, u32[]{:S(2)}) async-start(bf16[8,256,640]{2,1,0:T(8,128)(2,1)} %broadcast_in_dim.14), calls=%async_computation.2 | async-start | bytes 5242880 | tf_op jit(solution)/shard_map/all_to_all | solution.py:337
  111.4 8.9 %copy-start.38 = (f32[960]{0:T(1024)S(1)}, f32[960]{0:T(1024)}, u32[]{:S(2)}) copy-start(f32[960]{0:T(1024)} %param.22) | copy-start | bytes 11524
  111.4 384.5 %reduce-scatter.3.cloned.1.call-start = ((), (), s32[]{:S(2)}) async-start(), calls=%async_computation.11 | async-start | bytes 9469952 | tf_op jit(solution)/shard_map/reduce_scatter | solution.py:400
  115.5 87.6 %collective-permute-start.3 = (bf16[256,1024]{1,0:T(8,128)(2,1)}, bf16[256,1024]{1,0:T(8,128)(2,1)}, u32[]{:S(2)}, u32[]{:S(2)}) collective-permute-start(bf16[256,1024]{1,0:T(8,128)(2,1)} %bitcast.252), channel_id=1, source_target_pairs={{0,1},{1,0},{2,3},{3,2},{4,5},{5,4},{6,7},{7,6},{8,9},{9,8},{10,11... | collective-permute-start | bytes 1572872 | tf_op jit(solution)/shard_map/ppermute | solution.py:46
  131.7 59.9 %collective-permute-start = (bf16[8,60,1024]{2,0,1:T(8,128)(2,1)}, bf16[8,60,1024]{2,0,1:T(8,128)(2,1)}, u32[]{:S(2)}, u32[]{:S(2)}) collective-permute-start(bf16[8,60,1024]{2,0,1:T(8,128)(2,1)} %reshape.416), channel_id=1, source_target_pairs={{0,1},{1,0},{2,3},{3,2},{4,5},{5,4},{6,7},{7,6},{8,9},{9,8},{10,11... | collective-permute-start | bytes 2949128 | tf_op jit(solution)/shard_map/ppermute | solution.py:46
  202.2 39.3 %collective-permute-start.1 = (bf16[256,1024]{1,0:T(8,128)(2,1)}, bf16[256,1024]{1,0:T(8,128)(2,1)}, u32[]{:S(2)}, u32[]{:S(2)}) collective-permute-start(bf16[256,1024]{1,0:T(8,128)(2,1)} %multiply_convert_fusion.3), channel_id=1, source_target_pairs={{0,1},{1,0},{2,3},{3,2},{4,5},{5,4},{6,7},{7,6},{8,9},{9,8},{10,11... | collective-permute-start | bytes 1572872 | tf_op jit(solution)/shard_map/ppermute | solution.py:46
  253.6 10.7 %copy-start.31 = (f32[512,1024]{1,0:T(8,128)}, f32[512,1024]{1,0:T(8,128)S(1)}, u32[]{:S(2)}) copy-start(f32[512,1024]{1,0:T(8,128)S(1)} %fusion.43) | copy-start | bytes 6291460
  253.6 5.1 copy-start.18
  264.2 26.5 %collective-permute-start.4 = (bf16[256,1024]{1,0:T(8,128)(2,1)}, bf16[256,1024]{1,0:T(8,128)(2,1)}, u32[]{:S(2)}, u32[]{:S(2)}) collective-permute-start(bf16[256,1024]{1,0:T(8,128)(2,1)} %slice.331), channel_id=1, source_target_pairs={{0,1},{1,0},{2,3},{3,2},{4,5},{5,4},{6,7},{7,6},{8,9},{9,8},{10,11... | collective-permute-start | bytes 1572872 | tf_op jit(solution)/shard_map/ppermute | solution.py:46
  265.2 27.8 %collective-permute-start.2 = (bf16[256,1024]{1,0:T(8,128)(2,1)}, bf16[256,1024]{1,0:T(8,128)(2,1)}, u32[]{:S(2)}, u32[]{:S(2)}) collective-permute-start(bf16[256,1024]{1,0:T(8,128)(2,1)} %slice.332), channel_id=1, source_target_pairs={{0,1},{1,0},{2,3},{3,2},{4,5},{5,4},{6,7},{7,6},{8,9},{9,8},{10,11... | collective-permute-start | bytes 1572872 | tf_op jit(solution)/shard_map/ppermute | solution.py:46
  305.3 8.8 %collective-permute-start.8 = (bf16[8,60,1024]{2,0,1:T(8,128)(2,1)S(1)}, bf16[8,60,1024]{2,0,1:T(8,128)(2,1)S(1)}, u32[]{:S(2)}, u32[]{:S(2)}) collective-permute-start(bf16[8,60,1024]{2,0,1:T(8,128)(2,1)S(1)} %bitcast.297), channel_id=1, source_target_pairs={{0,1},{1,0},{2,3},{3,2},{4,5},{5,4},{6,7},{7,6},{8,9},{9,8},{10,11... | collective-permute-start | bytes 2949128 | tf_op jit(solution)/shard_map/ppermute | solution.py:46
  394.3 7.1 %copy-start.12 = (bf16[4096,640]{1,0:T(8,128)(2,1)S(1)}, bf16[4096,640]{1,0:T(8,128)(2,1)}, u32[]{:S(2)}) copy-start(bf16[4096,640]{1,0:T(8,128)(2,1)} %get-tuple-element.18) | copy-start | bytes 15728644
  396.4 5.0 collective-permute-start.5
  403.7 45.8 %all-to-all-start.5 = ((bf16[8,256,640]{2,1,0:T(8,128)(2,1)}), bf16[8,256,640]{2,1,0:T(8,128)(2,1)}, u32[]{:S(2)}, u32[]{:S(2)}) async-start(bf16[8,256,640]{2,1,0:T(8,128)(2,1)} %fusion), calls=%async_computation.5 | async-start | bytes 5242880 | tf_op jit(solution)/shard_map/all_to_all | solution.py:409
  415.0 37.1 %copy-start.24 = (bf16[15,64,256]{2,1,0:T(8,128)(2,1)}, bf16[15,64,256]{2,1,0:T(8,128)(2,1)S(1)}, u32[]{:S(2)}) copy-start(bf16[15,64,256]{2,1,0:T(8,128)(2,1)S(1)} %pad_maximum_fusion.10) | copy-start | bytes 1474564
  469.6 4.3 collective-permute-start.6
  472.6 1.3 collective-permute-start.7
  480.6 11.3 %copy-start.21 = (bf16[32,8,8,128]{3,1,2,0:T(8,128)(2,1)S(1)}, bf16[32,8,8,128]{3,1,2,0:T(8,128)(2,1)}, u32[]{:S(2)}) copy-start(bf16[32,8,8,128]{3,1,2,0:T(8,128)(2,1)} %get-tuple-element.42) | copy-start | bytes 1572868
  480.6 12.5 %copy-start.3 = (f32[256,1024]{1,0:T(8,128)S(1)}, f32[256,1024]{1,0:T(8,128)}, u32[]{:S(2)}) copy-start(f32[256,1024]{1,0:T(8,128)} %copy-done.2) | copy-start | bytes 3145732
  480.6 40.3 %all-to-all-start.6 = ((bf16[64,132,128]{2,1,0:T(8,128)(2,1)}), bf16[64,132,128]{2,1,0:T(8,128)(2,1)}, u32[]{:S(2)}, u32[]{:S(2)}) async-start(bf16[64,132,128]{2,1,0:T(8,128)(2,1)} %copy.370), calls=%async_computation.6 | async-start | bytes 4456448 | tf_op jit(solution)/shard_map/all_to_all | solution.py:436
  491.9 35.5 %reduce-scatter.5.cloned.1.call-start = ((), (), s32[]{:S(2)}) async-start(), calls=%async_computation.12 | async-start | bytes 696320 | tf_op jit(solution)/shard_map/reduce_scatter | solution.py:401
  (25 other events, 65.9 us)
Sparse Core Ops, SparseCore 0:
  29.5 90.4 all-gather.1
  332.4 89.5 reduce-scatter.2
  496.1 31.2 reduce-scatter.4

commit v2 on v1

v2 whole, which is shorter than its diff:
```python
import jax
import jax.numpy as jnp
from jax import lax
from jax.experimental import pallas as pl
from jax.experimental.pallas import tpu as pltpu
from jax.sharding import Mesh
from jax.sharding import PartitionSpec as P

D = 960
HEADS = 15
KV_HEADS = 5
GROUP = 3
HEAD_DIM = 64
SPAN = 128
PAD = 1024

EPS = 1e-05
ROPE_BASE = 100000.0

BF = jnp.bfloat16
F32 = jnp.float32

PLANE = ("y", "x")
LINE = ("zh", "zl")
CHIPS = ("zl", "y", "x", "zh")
SEQ = ("x", "zh")
SWAP = [(0, 1), (1, 0)]


def pad_width(value):
    rows = value.shape[0]
    blocks = value.reshape(rows, 8, 120)
    return jnp.pad(blocks, ((0, 0), (0, 0), (0, 8))).reshape(rows, PAD)


def cut_width(value):
    rows = value.shape[0]
    return value.reshape(rows, 8, 128)[:, :, :120].reshape(rows, D)


def pad_lanes(value):
    return jnp.pad(value, ((0, 0), (0, 128 - value.shape[1])))


def other_core(value):
    return lax.ppermute(value, "c", SWAP)


def dot_last(left, right):
    return lax.dot_general(left, right, (((1,), (1,)), ((), ())), preferred_element_type=F32)


def dot_first(left, right):
    return lax.dot_general(left, right, (((0,), (0,)), ((), ())), preferred_element_type=F32)


def dot_plain(left, right):
    return jnp.dot(left, right, preferred_element_type=F32)


VMEM_LIMIT = 56 * 1024 * 1024
WIDTH = GROUP * SPAN
TILES = 4
STEP = TILES * SPAN
SEQ_LEN = 4096
FEED = 640


def sort_blocks(info, sources, target):
    def one(slot, carry):
        at = pl.ds(pl.multiple_of(slot * SPAN, SPAN), SPAN)
        for n, source in enumerate(sources):
            to = pl.ds(pl.multiple_of(info[8 + 16 * n + slot] * SPAN, SPAN), SPAN)
            target[to, :] = source[at, :]
        return carry

    lax.fori_loop(0, 16, one, 0)


def unsort_blocks(info, source, targets):
    def one(slot, carry):
        at = pl.ds(pl.multiple_of(slot * SPAN, SPAN), SPAN)
        for n, target in enumerate(targets):
            to = pl.ds(pl.multiple_of(info[8 + 16 * n + slot] * SPAN, SPAN), SPAN)
            target[at, :] = source[to, :].astype(target.dtype)
        return carry

    lax.fori_loop(0, 16, one, 0)


def causal_steps(info, tile):
    low_half, low = info[0], info[1]
    high = 31 - low
    low_last = lax.div(low, TILES)
    high_last = lax.div(high, TILES)

    def whole(step, carry):
        is_low = step < low_last
        tile(
            jnp.where(is_low, low_half, 1 - low_half),
            jnp.where(is_low, step, step - low_last),
            None,
        )
        return carry

    lax.fori_loop(0, 7, whole, 0)
    tile(low_half, low_last, (low - low_last * TILES) * SPAN)
    tile(1 - low_half, high_last, (high - high_last * TILES) * SPAN)


def key_rows_minus_query_lanes():
    row = lax.broadcasted_iota(jnp.int32, (STEP, WIDTH), 0)
    lane = lax.broadcasted_iota(jnp.int32, (STEP, WIDTH), 1)
    return row - lax.rem(lane, SPAN)


def key_step(ref, step):
    return ref[pl.ds(pl.multiple_of(step * STEP, STEP), STEP), :]


def attend_kernel(info, mine_ref, other_ref, q_ref, out_ref, total_ref, keys_in_order, query, numer, total):
    sort_blocks(info, (mine_ref, other_ref), keys_in_order)
    query[...] = jnp.zeros_like(query)
    for half in range(2):
        query[half, :HEAD_DIM, :] = q_ref[0, half]
    numer[...] = jnp.zeros_like(numer)
    total[...] = jnp.zeros_like(total)

    def tile(half, step, limit):
        keys = key_step(keys_in_order, step)
        expo = jnp.exp(dot_plain(keys, query[half]))
        if limit is not None:
            expo = jnp.where(key_rows_minus_query_lanes() <= limit, expo, 0.0)
        numer[half] += dot_plain(keys.T[HEAD_DIM:], expo.astype(BF))
        total[half] += jnp.sum(expo.reshape(STEP // 8, 8, WIDTH), axis=0)

    causal_steps(info, tile)
    for half in range(2):
        summed = jnp.sum(total[half], axis=0, keepdims=True)
        total_ref[0, half] = summed
        out_ref[0, half] = numer[half] / summed


HEAD_SPEC = pl.BlockSpec((1, 2, HEAD_DIM, WIDTH), lambda g, s: (g, 0, 0, 0))
ROW_SPEC = pl.BlockSpec((1, 2, 1, WIDTH), lambda g, s: (g, 0, 0, 0))
KV_SPEC = pl.BlockSpec((SEQ_LEN // 2, 2 * HEAD_DIM), lambda g, s: (0, g))
HEAD_F32 = jax.ShapeDtypeStruct((KV_HEADS, 2, HEAD_DIM, WIDTH), F32)


def attend(info, mine, other, query):
    return pl.pallas_call(
        attend_kernel,
        grid_spec=pltpu.PrefetchScalarGridSpec(
            num_scalar_prefetch=1,
            grid=(KV_HEADS,),
            in_specs=[KV_SPEC, KV_SPEC, HEAD_SPEC],
            out_specs=[HEAD_SPEC, ROW_SPEC],
            scratch_shapes=[
                pltpu.VMEM((SEQ_LEN, 2 * HEAD_DIM), BF),
                pltpu.VMEM((2, 2 * HEAD_DIM, WIDTH), BF),
                pltpu.VMEM((2, HEAD_DIM, WIDTH), F32),
                pltpu.VMEM((2, 8, WIDTH), F32),
            ],
        ),
        out_shape=[HEAD_F32, jax.ShapeDtypeStruct((KV_HEADS, 2, 1, WIDTH), F32)],
        compiler_params=pltpu.CompilerParams(vmem_limit_bytes=VMEM_LIMIT),
        cost_estimate=pl.CostEstimate(flops=4 * 10**9, bytes_accessed=8 * 10**6, transcendentals=8 * 10**6),
    )(info, mine, other, query)


def attend_back_kernel(
    info, mine_ref, other_ref, q_ref, dnum_ref, delta_ref, dq_ref, dmine_ref, dother_ref, keys_in_order, wide, tall, dq, dkv
):
    sort_blocks(info, (mine_ref, other_ref), keys_in_order)
    for half in range(2):
        zero = jnp.zeros((HEAD_DIM, WIDTH), BF)
        both = jnp.concatenate(
            [
                jnp.concatenate([q_ref[0, half], zero], axis=1),
                jnp.concatenate([zero, dnum_ref[0, half]], axis=1),
            ],
            axis=0,
        )
        wide[half] = both
        tall[half] = both.T
    dq[...] = jnp.zeros_like(dq)
    dkv[...] = jnp.zeros_like(dkv)

    def tile(half, step, limit):
        keys = key_step(keys_in_order, step)
        scores = dot_plain(keys, wide[half])
        expo = jnp.exp(scores[:, :WIDTH])
        if limit is not None:
            expo = jnp.where(key_rows_minus_query_lanes() <= limit, expo, 0.0)
        grads = (expo * (scores[:, WIDTH:] - delta_ref[0, half])).astype(BF)
        pair = jnp.concatenate([grads, expo.astype(BF)], axis=1)
        at = pl.ds(pl.multiple_of(step * STEP, STEP), STEP)
        dkv[at, :] += dot_plain(pair, tall[half])
        dq[half] += dot_plain(keys.T[:HEAD_DIM], grads)

    causal_steps(info, tile)
    for half in range(2):
        dq_ref[0, half] = dq[half] * (HEAD_DIM**-0.5)
    unsort_blocks(info, dkv, (dmine_ref, dother_ref))


def attend_back(info, mine, other, query, dnum, delta):
    return pl.pallas_call(
        attend_back_kernel,
        grid_spec=pltpu.PrefetchScalarGridSpec(
            num_scalar_prefetch=1,
            grid=(KV_HEADS,),
            in_specs=[KV_SPEC, KV_SPEC, HEAD_SPEC, HEAD_SPEC, ROW_SPEC],
            out_specs=[HEAD_SPEC, KV_SPEC, KV_SPEC],
            scratch_shapes=[
                pltpu.VMEM((SEQ_LEN, 2 * HEAD_DIM), BF),
                pltpu.VMEM((2, 2 * HEAD_DIM, 2 * WIDTH), BF),
                pltpu.VMEM((2, 2 * WIDTH, 2 * HEAD_DIM), BF),
                pltpu.VMEM((2, HEAD_DIM, WIDTH), F32),
                pltpu.VMEM((SEQ_LEN, 2 * HEAD_DIM), F32),
            ],
        ),
        out_shape=[HEAD_F32] + [jax.ShapeDtypeStruct(mine.shape, BF)] * 2,
        compiler_params=pltpu.CompilerParams(vmem_limit_bytes=VMEM_LIMIT),
        cost_estimate=pl.CostEstimate(flops=10 * 10**9, bytes_accessed=12 * 10**6, transcendentals=8 * 10**6),
    )(info, mine, other, query, dnum, delta)


PARTS = ((0, 60), (64, 20), (88, 20))
BLOCK = 112


def project_kernel(info, mine_ref, other_ref, normed_ref, cos_ref, sin_ref, w_ref, query_ref, kv_ref, q_rows, k_rows, v_rows, pair):
    step = pl.program_id(0)
    core = info[2]
    for at in range(8):
        lanes = slice(at * 128, at * 128 + 128)
        w_ref[0, core, :, lanes] = mine_ref[at // 4, at % 4, 0, 0]
        w_ref[0, 1 - core, :, lanes] = other_ref[at // 4, at % 4, 0, 0]
    made = dot_last(w_ref[0].reshape(2 * BLOCK, PAD), normed_ref[...])
    for (start, count), rows in zip(PARTS, (q_rows, k_rows, v_rows)):
        pair[0:count] = made[start : start + count]
        pair[count : 2 * count] = made[BLOCK + start : BLOCK + start + count]
        rows[pl.ds(pl.multiple_of(step * 2 * count, 8), 2 * count), :] = pair[0 : 2 * count]

    @pl.when(step == 7)
    def _():
        cosine, sine = cos_ref[...], sin_ref[...]

        def turned(rows, head):
            first = rows[head * 64 : head * 64 + 32]
            second = rows[head * 64 + 32 : head * 64 + 64]
            return jnp.concatenate([first * cosine - second * sine, second * cosine + first * sine], axis=0)

        for g in range(KV_HEADS):
            for r in range(GROUP):
                head = turned(q_rows, GROUP * g + r).astype(BF) * BF(HEAD_DIM**-0.5)
                for half in range(2):
                    query_ref[g, half, :, r * SPAN : (r + 1) * SPAN] = head[:, half * SPAN : (half + 1) * SPAN]
            both = jnp.concatenate([turned(k_rows, g), v_rows[g * 64 : g * 64 + 64]], axis=0)
            kv_ref[:, g * 128 : (g + 1) * 128] = both.T.astype(BF)


def whole_spec(*shape):
    return pl.BlockSpec(shape, lambda j, s: (0,) * len(shape))


SMALL_SPEC = pl.BlockSpec((2, 4, 1, 1, BLOCK, 128), lambda j, s: (0, 0, j // 2, j % 2, 0, 0))
W_SPEC = pl.BlockSpec((1, 2, BLOCK, PAD), lambda j, s: (j, 0, 0, 0))


def project(info, mine, other, normed, cosine, sine):
    rows = normed.shape[0]
    return pl.pallas_call(
        project_kernel,
        grid_spec=pltpu.PrefetchScalarGridSpec(
            num_scalar_prefetch=1,
            grid=(8,),
            in_specs=[SMALL_SPEC, SMALL_SPEC, whole_spec(rows, PAD), whole_spec(32, rows), whole_spec(32, rows)],
            out_specs=[W_SPEC, whole_spec(KV_HEADS, 2, HEAD_DIM, WIDTH), whole_spec(rows, 640)],
            scratch_shapes=[
                pltpu.VMEM((D, rows), F32),
                pltpu.VMEM((320, rows), F32),
                pltpu.VMEM((320, rows), F32),
                pltpu.VMEM((120, rows), F32),
            ],
        ),
        out_shape=[
            jax.ShapeDtypeStruct((8, 2, BLOCK, PAD), BF),
            jax.ShapeDtypeStruct((KV_HEADS, 2, HEAD_DIM, WIDTH), BF),
            jax.ShapeDtypeStruct((rows, 640), BF),
        ],
        compiler_params=pltpu.CompilerParams(vmem_limit_bytes=VMEM_LIMIT),
        cost_estimate=pl.CostEstimate(flops=10**9, bytes_accessed=8 * 10**6, transcendentals=0),
    )(info, mine, other, normed, cosine, sine)


def project_back_kernel(
    info, dq_ref, dkv_ref, normed_ref, cos_ref, sin_ref, w_ref, dn_ref, mine_ref, other_ref, q_rows, k_rows, v_rows, pair, blocks, grads
):
    step = pl.program_id(0)
    core = info[2]

    @pl.when(step == 0)
    def _():
        cosine, sine = cos_ref[...], sin_ref[...]

        def turned_back(value):
            first, second = value[:32], value[32:]
            return jnp.concatenate([first * cosine + second * sine, second * cosine - first * sine], axis=0)

        for g in range(KV_HEADS):
            for r in range(GROUP):
                lanes = slice(r * SPAN, (r + 1) * SPAN)
                head = jnp.concatenate([dq_ref[g, 0, :, lanes], dq_ref[g, 1, :, lanes]], axis=1)
                at = (GROUP * g + r) * 64
                q_rows[at : at + 64] = turned_back(head)
            both = dkv_ref[:, g * 128 : (g + 1) * 128].T
            k_rows[g * 64 : g * 64 + 64] = turned_back(both[:64])
            v_rows[g * 64 : g * 64 + 64] = both[64:]
        blocks[...] = jnp.zeros_like(blocks)
        dn_ref[...] = jnp.zeros_like(dn_ref)

    for (start, count), rows in zip(PARTS, (q_rows, k_rows, v_rows)):
        pair[0 : 2 * count] = rows[pl.ds(pl.multiple_of(step * 2 * count, 8), 2 * count), :]
        blocks[start : start + count] = pair[0:count]
        blocks[BLOCK + start : BLOCK + start + count] = pair[count : 2 * count]
    block = blocks[...].astype(BF)
    dn_ref[...] += dot_first(block, w_ref[0].reshape(2 * BLOCK, PAD))
    grads[...] = dot_plain(block, normed_ref[...]).astype(BF).reshape(2, BLOCK, PAD)
    for at in range(8):
        lanes = slice(at * 128, at * 128 + 128)
        mine_ref[at // 4, at % 4, 0, 0] = grads[core, :, lanes]
        other_ref[at // 4, at % 4, 0, 0] = grads[1 - core, :, lanes]


def project_back(info, dq, dkv, normed, cosine, sine, w_all):
    rows = normed.shape[0]
    small = jax.ShapeDtypeStruct((2, 4, 4, 2, BLOCK, 128), BF)
    return pl.pallas_call(
        project_back_kernel,
        grid_spec=pltpu.PrefetchScalarGridSpec(
            num_scalar_prefetch=1,
            grid=(8,),
            in_specs=[
                whole_spec(KV_HEADS, 2, HEAD_DIM, WIDTH),
                whole_spec(rows, 640),
                whole_spec(rows, PAD),
                whole_spec(32, rows),
                whole_spec(32, rows),
                W_SPEC,
            ],
            out_specs=[whole_spec(rows, PAD), SMALL_SPEC, SMALL_SPEC],
            scratch_shapes=[
                pltpu.VMEM((D, rows), F32),
                pltpu.VMEM((320, rows), F32),
                pltpu.VMEM((320, rows), F32),
                pltpu.VMEM((120, rows), F32),
                pltpu.VMEM((2 * BLOCK, rows), F32),
                pltpu.VMEM((2, BLOCK, PAD), BF),
            ],
        ),
        out_shape=[jax.ShapeDtypeStruct((rows, PAD), F32), small, small],
        compiler_params=pltpu.CompilerParams(vmem_limit_bytes=VMEM_LIMIT),
        cost_estimate=pl.CostEstimate(flops=2 * 10**9, bytes_accessed=10 * 10**6, transcendentals=0),
    )(info, dq, dkv, normed, cosine, sine, w_all)


def feed_kernel(
    gate_ref, up_ref, down_ref, n_mine, n_other, dy_mine, dy_other,
    fed_mine, fed_other, dn_mine, dn_other, grad_ref, normed, dy, wg, wu, wd, fed, dn
):
    step = pl.program_id(0)
    rows = n_mine.shape[0]

    @pl.when(step == 0)
    def _():
        normed[:rows] = n_mine[...]
        normed[rows:] = n_other[...]
        dy[:rows] = dy_mine[...]
        dy[rows:] = dy_other[...]
        fed[...] = jnp.zeros_like(fed)
        dn[...] = jnp.zeros_like(dn)

    for group in range(4):
        part = slice(group * 160, group * 160 + 160)
        for at in range(8):
            lanes = slice(at * 128, at * 128 + 128)
            wg[part, lanes] = gate_ref[at % 4, group // 2, group % 2, at // 4]
            wu[part, lanes] = up_ref[at % 4, group // 2, group % 2, at // 4]
            wd[part, lanes] = down_ref[group, at // 2, at % 2, 0]
    gate = dot_last(normed[...], wg[...])
    upward = dot_last(normed[...], wu[...])
    dact = dot_last(dy[...], wd[...])
    sigma = jax.nn.sigmoid(gate)
    silu_gate = gate * sigma
    active = (silu_gate * upward).astype(BF)
    dgate = (dact * upward * sigma * (1.0 + gate * (1.0 - sigma))).astype(BF)
    dup = (dact * silu_gate).astype(BF)
    fed[...] += dot_plain(active, wd[...])
    dn[...] += dot_plain(dgate, wg[...]) + dot_plain(dup, wu[...])
    g_gate = dot_first(dgate, normed[...]).astype(BF)
    g_up = dot_first(dup, normed[...]).astype(BF)
    g_down = dot_first(active, dy[...]).astype(BF)
    for group in range(4):
        part = slice(group * 160, group * 160 + 160)
        for at in range(8):
            lanes = slice(at * 128, at * 128 + 128)
            grad_ref[at % 4, 2 * step + group // 2, group % 2, at // 4, 0:160] = g_gate[part, lanes]
            grad_ref[at % 4, 2 * step + group // 2, group % 2, at // 4, 160:320] = g_up[part, lanes]
            grad_ref[group, at // 2, at % 2, step, 320:480] = g_down[part, lanes]

    @pl.when(step == 1)
    def _():
        fed_mine[...] = fed[:rows]
        fed_other[...] = fed[rows:].astype(BF)
        dn_mine[...] = dn[:rows]
        dn_other[...] = dn[rows:].astype(BF)


def feed(big, n_mine, n_other, dy_mine, dy_other):
    rows = n_mine.shape[0]
    by_plane = (4, 2, 2, 2, 160, 128)

    def flat(*shape):
        return pl.BlockSpec(shape, lambda k: (0,) * len(shape))

    return pl.pallas_call(
        feed_kernel,
        grid=(2,),
        in_specs=[
            pl.BlockSpec(by_plane, lambda k: (0, k, 0, 0, 0, 0)),
            pl.BlockSpec(by_plane, lambda k: (0, k, 0, 0, 1, 0)),
            pl.BlockSpec((4, 4, 2, 1, 160, 128), lambda k: (0, 0, 0, k, 2, 0)),
        ]
        + [flat(rows, PAD)] * 4,
        out_specs=[flat(rows, PAD)] * 4 + [flat(4, 4, 2, 2, 480, 128)],
        out_shape=[
            jax.ShapeDtypeStruct((rows, PAD), F32),
            jax.ShapeDtypeStruct((rows, PAD), BF),
            jax.ShapeDtypeStruct((rows, PAD), F32),
            jax.ShapeDtypeStruct((rows, PAD), BF),
            jax.ShapeDtypeStruct((4, 4, 2, 2, 480, 128), BF),
        ],
        scratch_shapes=[pltpu.VMEM((2 * rows, PAD), BF)] * 2
        + [pltpu.VMEM((FEED, PAD), BF)] * 3
        + [pltpu.VMEM((2 * rows, PAD), F32)] * 2,
        compiler_params=pltpu.CompilerParams(vmem_limit_bytes=VMEM_LIMIT),
        cost_estimate=pl.CostEstimate(flops=12 * 10**9, bytes_accessed=22 * 10**6, transcendentals=10**6),
    )(big, big, big, n_mine, n_other, dy_mine, dy_other)


def by_half(value):
    rows = value.shape[1]
    split = value.reshape(KV_HEADS, GROUP, rows, 2, SPAN)
    return split.transpose(0, 3, 2, 1, 4).reshape(KV_HEADS, 2, rows, WIDTH)


def by_head(value):
    rows = value.shape[2]
    split = value.reshape(KV_HEADS, 2, rows, GROUP, SPAN)
    return split.transpose(0, 3, 2, 1, 4).reshape(HEADS, rows, 2 * SPAN)


def pad_rows(value, count):
    return jnp.pad(value, ((0, count - value.shape[0]), (0, 0)))


def norm_forward(value, gain):
    inverse = lax.rsqrt(jnp.sum(value * value, axis=-1, keepdims=True) / D + EPS)
    unit = value * inverse
    return unit, inverse, (unit * gain).astype(BF)


def norm_back(grad, unit, inverse, gain):
    scaled = grad * gain
    inner = jnp.sum(scaled * unit, axis=-1, keepdims=True) / D
    return inverse * (scaled - unit * inner), jnp.sum(grad * unit, axis=0)


def body(
    tokens,
    w_query,
    w_key,
    w_value,
    w_out,
    w_gate,
    w_up,
    w_down,
    attention_norm_gain,
    feedforward_norm_gain,
    span_order,
    positions,
    out_grad,
):
    rows = tokens.shape[0]
    core = lax.axis_index("c")
    me = lax.axis_index(("x", "zh", "c"))

    small = jnp.concatenate([pad_rows(w_query.T, 64), pad_rows(w_key.T, 24), pad_rows(w_value.T, 24)], axis=0)
    small = lax.all_to_all(jnp.broadcast_to(pad_lanes(small), (64, BLOCK, 128)), CHIPS, 0, 0, tiled=True)
    small = small.reshape(2, 4, 4, 2, BLOCK, 128)

    mixed = jnp.concatenate([w_down.reshape(2, 160, 60), w_out.reshape(2, 60, 60)], axis=1)
    mixed = lax.all_to_all(mixed, "c", 0, 0, tiled=True)
    mixed = jnp.concatenate([mixed[0], mixed[1]], axis=1)
    big = jnp.concatenate([w_gate.T, w_up.T, mixed], axis=0)
    big = pad_rows(pad_lanes(big), 544)
    big = lax.all_to_all(jnp.broadcast_to(big, (4, 544, 128)), LINE, 0, 0, tiled=True)
    big = lax.all_gather(big, PLANE, axis=0, tiled=True).reshape(4, 4, 2, 2, 544, 128)

    order = span_order[0]
    own_pair = lax.dynamic_slice_in_dim(order, 2 * me, 2)
    own_low_half = (own_pair[0] > own_pair[1]).astype(jnp.int32)
    spans = order.reshape(8, 2, 2)
    info = jnp.concatenate(
        [
            jnp.stack([own_low_half, jnp.minimum(own_pair[0], own_pair[1]), core.astype(jnp.int32)]),
            jnp.zeros((5,), jnp.int32),
            lax.dynamic_index_in_dim(spans, core, 1, keepdims=False).reshape(16),
            lax.dynamic_index_in_dim(spans, 1 - core, 1, keepdims=False).reshape(16),
        ]
    ).astype(jnp.int32)
    place = jnp.concatenate(
        [
            lax.dynamic_slice_in_dim(positions[0], own_pair[0] * SPAN, SPAN, 0),
            lax.dynamic_slice_in_dim(positions[0], own_pair[1] * SPAN, SPAN, 0),
        ]
    )
    half_dim = HEAD_DIM // 2
    freq = jnp.power(ROPE_BASE, -jnp.arange(half_dim, dtype=F32) / half_dim)
    angle = freq[:, None] * place.astype(F32)[None, :]
    cosine, sine = jnp.cos(angle), jnp.sin(angle)

    gain_one = pad_width(attention_norm_gain[None])
    gain_two = pad_width(feedforward_norm_gain[None])
    layer_input = pad_width(tokens).astype(F32)
    dy = pad_width(out_grad)
    dy_other = other_core(dy)

    unit_one, inverse_one, normed_one = norm_forward(layer_input, gain_one)
    w_all, query, kv_local = project(info, small, other_core(small), normed_one, cosine, sine)

    kv = lax.all_to_all(jnp.broadcast_to(kv_local, (8, rows, 640)), SEQ, 0, 0, tiled=True)
    kv = kv.reshape(8 * rows, 640)
    kv_other = other_core(kv)

    attended, total = attend(info, kv, kv_other, query)
    attended = by_head(attended)
    total = by_head(total)
    attended_low = attended.astype(BF).reshape(16, 60, rows)
    attended_low = jnp.pad(attended_low, ((0, 0), (0, 4), (0, 0))).reshape(PAD, rows)

    w_out_h = big[:, :, :, :, 480:].transpose(3, 0, 4, 1, 2, 5).reshape(8, 64, PAD)
    w_out_o = other_core(w_out_h)
    first = core == 0
    w_out_full = jnp.stack(
        [jnp.where(first, w_out_h, w_out_o), jnp.where(first, w_out_o, w_out_h)], axis=1
    ).reshape(PAD, PAD)

    hidden = layer_input + dot_first(attended_low, w_out_full)
    unit_two, inverse_two, normed_two = norm_forward(hidden, gain_two)
    fed, fed_other, dn_two, dn_other, g_big = feed(big, normed_two, other_core(normed_two), dy, dy_other)
    dn_two = dn_two + other_core(dn_other).astype(F32)
    result = cut_width((hidden + (fed + other_core(fed_other).astype(F32))).astype(BF))

    back_two, gain_two_grad = norm_back(dn_two, unit_two, inverse_two, gain_two)
    dh = dy.astype(F32) + back_two
    dh_low = dh.astype(BF)
    dob = dot_last(w_out_full, dh_low).astype(BF).reshape(16, 64, rows)[:, :60]
    dob = dob.reshape(HEADS, HEAD_DIM, rows).astype(F32)
    dnum = (dob / total).astype(BF)
    delta = jnp.sum(dob * attended, axis=1, keepdims=True) / total

    g_big = lax.psum_scatter(g_big.reshape(64 * 480, 128), PLANE, scatter_dimension=0, tiled=True)
    g_big = lax.psum_scatter(g_big, LINE, scatter_dimension=0, tiled=True)

    g_out = dot_plain(attended_low, dh_low).astype(BF).reshape(8, 2, 64, PAD)
    keep = lax.dynamic_index_in_dim(g_out, core, 1, keepdims=False)
    give = lax.dynamic_index_in_dim(g_out, 1 - core, 1, keepdims=False)
    g_out = (keep.astype(F32) + other_core(give).astype(F32)).astype(BF)
    g_out = g_out.reshape(8, 64, 8, 128).transpose(0, 2, 1, 3).reshape(64, 64, 128)
    g_out = lax.all_to_all(g_out, CHIPS, 0, 0, tiled=True)
    g_out = jnp.sum(g_out.astype(F32), axis=0)

    dq, dkv, dkv_other = attend_back(info, kv, kv_other, query, by_half(dnum), by_half(delta))
    dkv = (dkv.astype(F32) + other_core(dkv_other).astype(F32)).astype(BF)
    dkv = lax.all_to_all(dkv.reshape(8, rows, 640), SEQ, 0, 0, tiled=True)
    dkv = jnp.sum(dkv.astype(F32), axis=0)

    dn_one, g_small, g_other = project_back(info, dq, dkv, normed_one, cosine, sine, w_all)
    back_one, gain_one_grad = norm_back(dn_one, unit_one, inverse_one, gain_one)
    input_grad = cut_width((dh + back_one).astype(BF))

    g_small = (g_small.astype(F32) + other_core(g_other).astype(F32)).astype(BF).reshape(64, BLOCK, 128)
    gains = jnp.stack([gain_one_grad, gain_two_grad])
    gains = gains + other_core(gains)
    gains_high = gains.astype(BF)
    gains_low = (gains - gains_high.astype(F32)).astype(BF)
    gains = jnp.concatenate([gains_high.reshape(16, 128), gains_low.reshape(16, 128)], axis=0)
    last = jnp.concatenate([g_small, jnp.broadcast_to(gains, (64, 32, 128))], axis=1)
    last = lax.all_to_all(last, CHIPS, 0, 0, tiled=True)
    last = jnp.sum(last.astype(F32), axis=0)
    gains = cut_width((last[BLOCK : BLOCK + 16] + last[BLOCK + 16 :]).reshape(2, PAD))

    g_big = g_big.astype(F32)
    mixed = jnp.concatenate([g_big[320:480, :120], g_out[:60, :120]], axis=0)
    mixed = mixed.reshape(220, 2, 60).transpose(1, 0, 2)
    mixed = lax.all_to_all(mixed, "c", 0, 0, tiled=True)
    return (
        result,
        input_grad,
        last[:60, :120].T,
        last[64:84, :120].T,
        last[88:108, :120].T,
        mixed[:, 160:].reshape(120, 60),
        g_big[:160, :120].T,
        g_big[160:320, :120].T,
        mixed[:, :160].reshape(320, 60),
        gains[0],
        gains[1],
    )


def solution(mesh):
    fine = Mesh(mesh.devices.reshape(2, 4, 4, 2, 2), ("zl", "y", "x", "zh", "c"))
    shard, ctx = ("zl", "y"), ("x", "zh", "c")
    both = shard + ctx
    return jax.shard_map(
        body,
        mesh=fine,
        in_specs=(P(both, None),)
        + (P(shard, ctx),) * 7
        + (P(), P(), P(shard, None), P(shard, None), P(both, None)),
        out_specs=(P(both, None), P(both, None)) + (P(shard, ctx),) * 7 + (P(), P()),
        check_vma=False,
    )
```

time: 551 us -> 435 us (0.79)
  local copies, waits for them, and re-layouts: 193 us -> 37.3 us
  blocking collectives: 40.3 us -> 110 us
  matrix products: 40.6 us -> 2.32 us
  Pallas kernels: 81.7 us -> 105 us
  waiting for transfers between devices: 103 us -> 82.8 us
  other arithmetic: 26.3 us -> 32.3 us
    all_to_all x2 -> x3, blocking collectives: 21.8 us -> 105 us  [the longest x1 50.4 us: body(): lax.all_to_all(jnp.broadcast_to(kv_local, (8, rows, 640)), SEQ, 0, 0, til...]
    reshape x20 -> x6, local copies, waits for them, and re-layouts: 64.5 us -> 2.75 us  [the longest x2 1.81 us: by_half(): return split.transpose(0, 3, 2, 1, 4).reshape(KV_HEADS, 2, rows, WIDTH)]
    pallas_call x0 -> x3, Pallas kernels: none -> 42.8 us  [the longest x1 22.9 us: feed(): pl.pallas_call(feed_kernel, grid=(2,), in_specs=[pl.BlockSpec(by_plane, l...]
    transpose x14 -> x6, local copies, waits for them, and re-layouts: 33 us -> 4.75 us  [the longest x2 2.39 us: body(): big[:, :, :, :, 480:].transpose(3, 0, 4, 1, 2, 5).reshape(8, 64, PAD)]
    unnamed x96 -> x50, local copies, waits for them, and re-layouts: 31.3 us -> 9.08 us
    all_to_all x3 -> x2, waiting for transfers between devices: 70.4 us -> 48.7 us  [the longest x1 38.5 us: body(): dkv = lax.all_to_all(dkv.reshape(8, rows, 640), SEQ, 0, 0, tiled=True)]
    dot_general x5 -> x1, matrix products: 18.1 us -> 0.86 us  [dot_first(): lax.dot_general(left, right, (((0,), (0,)), ((), ())), preferred_element_...]
    pallas_call x1, Pallas kernels: 54 us -> 38.3 us  [attend_back(): pl.pallas_call(attend_back_kernel, grid_spec=pltpu.PrefetchScalarGridSpec...]
  transfers between devices with their start and end apart: 17 -> 18, of which waited for: 7 -> 8; matrix products, arithmetic and copies ran while one was open for 35% -> 14% of each run, Pallas kernels for 15% -> 19%
where the time goes in v2:
time: 435 us; the launch traced here: 427 us
  blocking collectives  110 us (25%)
  Pallas kernels  105 us (24%)
  waiting for transfers between devices  82.8 us (19%)
  starting transfers between devices  37.9 us (9%)
  local copies, waits for them, and re-layouts  37.3 us (9%)
  other arithmetic  32.3 us (7%)
  between operations  18.8 us (4%)
    all_to_all x1, blocking collectives, body(): lax.all_to_all(jnp.broadcast_to(kv_local, (8, rows, 640)), SEQ, 0, 0, til...  50.4 us
    all_to_all x1, blocking collectives, body(): lax.all_to_all(jnp.broadcast_to(pad_lanes(small), (64, BLOCK, 128)), CHIP...  40.1 us
    all_to_all x1, waiting for transfers between devices, body(): dkv = lax.all_to_all(dkv.reshape(8, rows, 640), SEQ, 0, 0, tiled=True)  38.5 us
    pallas_call x1, Pallas kernels, attend_back(): pl.pallas_call(attend_back_kernel, grid_spec=pltpu.PrefetchScalarGridSpec...  38.3 us
    pallas_call x1, Pallas kernels, attend(): pl.pallas_call(attend_kernel, grid_spec=pltpu.PrefetchScalarGridSpec(num_...  23.8 us
    pallas_call x1, Pallas kernels, feed(): pl.pallas_call(feed_kernel, grid=(2,), in_specs=[pl.BlockSpec(by_plane, l...  22.9 us
    all_to_all x1, waiting for transfers between devices, body(): last = lax.all_to_all(last, CHIPS, 0, 0, tiled=True)  22.1 us
    all_to_all x1, blocking collectives, body(): lax.all_to_all(jnp.broadcast_to(big, (4, 544, 128)), LINE, 0, 0, tiled=True)  14.4 us
  transfers between devices with their start and end apart: 18, of which 8 were waited for; matrix products, arithmetic and copies ran while one was open for 14% of the time, Pallas kernels for 19%

profile of v2, /device:TPU:1, one launch (start us, length us, event | category | flops | bytes accessed | tf_op | source)
XLA Modules:
  0.0 426.6 jit_solution(4807435116443977814)
XLA Ops:
  9.7 4.7 %all-to-all-start.2 = ((bf16[2,220,60]{1,2,0:T(8,128)(2,1)}), bf16[2,220,60]{1,2,0:T(8,128)(2,1)S(1)}, u32[]{:S(2)}, u32[]{:S(2)}) async-start(bf16[2,220,60]{1,2,0:T(8,128)(2,1)} %copy.132), calls=%async_computation.2 | async-start | bytes 131072 | tf_op jit(solution)/shard_map/all_to_all | solution.py:505
  16.6 14.4 %all_to_all.40 = bf16[4,544,128]{2,1,0:T(8,128)(2,1)} all-to-all(bf16[4,544,128]{2,1,0:T(8,128)(2,1)S(1)} %broadcast_in_dim.10), channel_id=1, replica_groups=mesh['zl'=2,'y'=4,'x'=4,'zh'=2,'c'=2] {'zh','zl'}, dimensions={0} | all-to-all | bytes 1114112 | tf_op jit(solution)/shard_map/all_to_all | solution.py:509
  31.4 40.1 %all_to_all.41 = bf16[64,112,128]{2,1,0:T(8,128)(2,1)S(1)} all-to-all(bf16[64,112,128]{2,1,0:T(8,128)(2,1)S(1)} %broadcast_in_dim.8), channel_id=1, replica_groups=mesh['zl'=2,'y'=4,'x'=4,'zh'=2,'c'=2] {'zl','y','x','zh'}, dimensions={0} | all-to-all | bytes 3670016 | tf_op jit(solution)/shard_map/all_to_all | solution.py:501
  71.5 4.4 %collective-permute-start = (bf16[2,4,4,2,112,128]{5,4,3,2,1,0:T(8,128)(2,1)S(1)}, bf16[2,4,4,2,112,128]{5,4,3,2,1,0:T(8,128)(2,1)}, u32[]{:S(2)}, u32[]{:S(2)}) collective-permute-start(bf16[2,4,4,2,112,128]{5,4,3,2,1,0:T(8,128)(2,1)S(1)} %bitcast.167), channel_id=1, source_target_pairs={{0,1},{1,0},{2,3},{3,2},{4,5},{5,4},{6,7},{7,6},{8,9},{9,8},{10,11... | collective-permute-start | bytes 5505032 | tf_op jit(solution)/shard_map/ppermute | solution.py:46
  86.7 9.5 %shard_map.212 = (bf16[8,2,112,1024]{3,2,1,0:T(8,128)(2,1)}, bf16[5,2,64,384]{3,2,1,0:T(8,128)(2,1)}, bf16[256,640]{1,0:T(8,128)(2,1)}) custom-call(s32[40]{0:T(128)} %concatenate.35.info, bf16[2,4,4,2,112,128]{5,4,3,2,1,0:T(8,128)(2,1)} %bitcast.168, bf16[2,4,4,2,112,128]{5,4,3,2,1,0:T(8,128)(2,1)} %collective-permute-done.other_ref, ...), custom_call_target="tpu_custom_call" | custom-call | flops 1000000000 | bytes 8000000 | tf_op jit(solution)/shard_map/pallas_call | solution.py:274
  97.4 50.4 %all_to_all.42 = bf16[8,256,640]{2,1,0:T(8,128)(2,1)} all-to-all(bf16[8,256,640]{2,1,0:T(8,128)(2,1)S(1)} %broadcast_in_dim.9), channel_id=1, replica_groups=mesh['zl'=2,'y'=4,'x'=4,'zh'=2,'c'=2] {'x','zh'}, dimensions={0} | all-to-all | bytes 5242880 | tf_op jit(solution)/shard_map/all_to_all | solution.py:544
  155.7 23.8 %shard_map.213 = (f32[5,2,64,384]{3,2,1,0:T(8,128)}, f32[5,2,1,384]{3,2,1,0:T(1,128)}) custom-call(s32[40]{0:T(128)} %concatenate.35.info, bf16[2048,640]{1,0:T(8,128)(2,1)} %bitcast.13.mine_ref, bf16[2048,640]{1,0:T(8,128)(2,1)} %collective-permute-done.1.other_ref, bf16[5,2,64,384]{3,2,1,0:T(8,128)(2,1)} %get-tuple-element.28.q_ref), custom_call_target="tpu_custom_call" | custom-call | flops 4000000000 | bytes 8000000 | tf_op jit(solution)/shard_map/pallas_call | solution.py:151
  185.3 1.9 collective-permute-done.3.n_other
  188.0 22.9 %shard_map.214 = (f32[256,1024]{1,0:T(8,128)}, bf16[256,1024]{1,0:T(8,128)(2,1)}, f32[256,1024]{1,0:T(8,128)}, bf16[256,1024]{1,0:T(8,128)(2,1)}, bf16[4,4,2,2,480,128]{5,4,3,2,1,0:T(8,128)(2,1)}) custom-call(bf16[4,4,2,2,544,128]{5,4,3,2,1,0:T(8,128)(2,1)} %bitcast.191, bf16[4,4,2,2,544,128]{5,4,3,2,1,0:T(8,128)(2,1)} %bitcast.192, ...), custom_call_target="tpu_custom_call" | custom-call | flops 12000000000 | bytes 22000000 | tf_op jit(solution)/shard_map/pallas_call | solution.py:428
  214.8 2.8 multiply_add_fusion
  219.5 1.7 reshape.255
  225.2 38.3 %shard_map.215 = (f32[5,2,64,384]{3,2,1,0:T(8,128)}, bf16[2048,640]{1,0:T(8,128)(2,1)}, bf16[2048,640]{1,0:T(8,128)(2,1)}) custom-call(s32[40]{0:T(128)} %concatenate.35.info, bf16[2048,640]{1,0:T(8,128)(2,1)} %bitcast.13.mine_ref, bf16[2048,640]{1,0:T(8,128)(2,1)} %collective-permute-done.1.other_ref, bf16[5,2,64,384]{3,2,1,0:T(8,128)(2,1)} %get-tuple-element.28.q_ref, ...), custom_call_target="tpu_custom_call" | custom-call | flops 10000000000 | bytes 12000000 | tf_op jit(solution)/shard_map/pallas_call | solution.py:208
  263.6 5.0 %collective-permute-done.7 = bf16[2048,640]{1,0:T(8,128)(2,1)S(1)} collective-permute-done((bf16[2048,640]{1,0:T(8,128)(2,1)}, bf16[2048,640]{1,0:T(8,128)(2,1)S(1)}, u32[]{:S(2)}, u32[]{:S(2)}) %collective-permute-start.7) | collective-permute-done | bytes 2621472 | tf_op jit(solution)/shard_map/ppermute | solution.py:46
  268.6 4.0 add_convert_fusion
  272.6 4.5 %all-to-all-start.4 = ((bf16[8,256,640]{2,1,0:T(8,128)(2,1)}), bf16[8,256,640]{2,1,0:T(8,128)(2,1)}, u32[]{:S(2)}, u32[]{:S(2)}) async-start(bf16[8,256,640]{2,1,0:T(8,128)(2,1)} %bitcast.161), calls=%async_computation.4 | async-start | bytes 5242880 | tf_op jit(solution)/shard_map/all_to_all | solution.py:588
  279.6 38.5 %all-to-all-done.4 = bf16[8,256,640]{2,1,0:T(8,128)(2,1)} async-done(((bf16[8,256,640]{2,1,0:T(8,128)(2,1)}), bf16[8,256,640]{2,1,0:T(8,128)(2,1)}, u32[]{:S(2)}, u32[]{:S(2)}) %all-to-all-start.4) | async-done | bytes 2621472 | tf_op jit(solution)/shard_map/all_to_all | solution.py:588
  318.1 3.0 convert_reduce_fusion.dkv_ref
  321.0 10.4 %shard_map.216 = (f32[256,1024]{1,0:T(8,128)}, bf16[2,4,4,2,112,128]{5,4,3,2,1,0:T(8,128)(2,1)}, bf16[2,4,4,2,112,128]{5,4,3,2,1,0:T(8,128)(2,1)}) custom-call(s32[40]{0:T(128)} %concatenate.35.info, f32[5,2,64,384]{3,2,1,0:T(8,128)} %get-tuple-element.35.dq_ref, f32[256,640]{1,0:T(8,128)} %convert_reduce_fusion.dkv_ref, ...), custom_call_target="tpu_custom_call" | custom-call | flops 2000000000 | bytes 10000000 | tf_op jit(solution)/shard_map/pallas_call | solution.py:340
  332.0 1.7 fusion
  335.3 14.3 %all-to-all-start.6 = ((bf16[64,64,128]{2,1,0:T(8,128)(2,1)}), bf16[64,64,128]{2,1,0:T(8,128)(2,1)S(1)}, u32[]{:S(2)}, u32[]{:S(2)}) async-start(bf16[64,64,128]{2,1,0:T(8,128)(2,1)} %bitcast.174), calls=%async_computation.8 | async-start | bytes 2097152 | tf_op jit(solution)/shard_map/all_to_all | solution.py:583
  349.6 1.7 multiply_reduce_fusion.1
  352.7 2.5 add_convert_fusion.1
  355.3 1.6 pad_maximum_fusion
  356.9 10.2 %all-to-all-done.6 = bf16[64,64,128]{2,1,0:T(8,128)(2,1)S(1)} async-done(((bf16[64,64,128]{2,1,0:T(8,128)(2,1)}), bf16[64,64,128]{2,1,0:T(8,128)(2,1)S(1)}, u32[]{:S(2)}, u32[]{:S(2)}) %all-to-all-start.6) | async-done | bytes 1048608 | tf_op jit(solution)/shard_map/all_to_all | solution.py:583
  367.1 6.2 %all-to-all-start.5 = ((bf16[64,144,128]{2,1,0:T(8,128)(2,1)}), bf16[64,144,128]{2,1,0:T(8,128)(2,1)}, u32[]{:S(2)}, u32[]{:S(2)}) async-start(bf16[64,144,128]{2,1,0:T(8,128)(2,1)} %pad_maximum_fusion), calls=%async_computation.5 | async-start | bytes 4718592 | tf_op jit(solution)/shard_map/all_to_all | solution.py:602
  373.4 1.9 copy.154
  375.4 2.1 copy.137
  377.7 1.6 fusion.5
  380.5 22.1 %all-to-all-done.5 = bf16[64,144,128]{2,1,0:T(8,128)(2,1)} async-done(((bf16[64,144,128]{2,1,0:T(8,128)(2,1)}), bf16[64,144,128]{2,1,0:T(8,128)(2,1)}, u32[]{:S(2)}, u32[]{:S(2)}) %all-to-all-start.5) | async-done | bytes 2359328 | tf_op jit(solution)/shard_map/all_to_all | solution.py:602
  402.6 2.0 convert_reduce_fusion.1
  407.2 2.8 reduce-scatter.5.cloned.1.call-done
  412.5 5.4 %all_to_all.43 = f32[2,220,60]{1,2,0:T(8,128)S(1)} all-to-all(f32[2,220,60]{1,2,0:T(8,128)S(1)} %bitcast.181), channel_id=1, replica_groups=mesh['zl'=2,'y'=4,'x'=4,'zh'=2,'c'=2] {'c'}, dimensions={0} | all-to-all | bytes 211200 | tf_op jit(solution)/shard_map/all_to_all | solution.py:609
  (167 shorter events, 51.3 us)
Async XLA Ops:
  7.2 23.9 %copy-start.15 = (bf16[120,20]{0,1:T(8,128)(2,1)S(1)}, bf16[120,20]{0,1:T(8,128)(2,1)}, u32[]{:S(2)}) copy-start(bf16[120,20]{0,1:T(8,128)(2,1)} %param.16) | copy-start | bytes 14404
  7.2 23.9 %copy-start.16 = (bf16[120,20]{0,1:T(8,128)(2,1)S(1)}, bf16[120,20]{0,1:T(8,128)(2,1)}, u32[]{:S(2)}) copy-start(bf16[120,20]{0,1:T(8,128)(2,1)} %param.15) | copy-start | bytes 14404
  7.2 23.9 %copy-start.13 = (bf16[120,60]{0,1:T(8,128)(2,1)S(1)}, bf16[120,60]{0,1:T(8,128)(2,1)}, u32[]{:S(2)}) copy-start(bf16[120,60]{0,1:T(8,128)(2,1)} %param.14) | copy-start | bytes 43204
  9.7 6.5 %all-to-all-start.2 = ((bf16[2,220,60]{1,2,0:T(8,128)(2,1)}), bf16[2,220,60]{1,2,0:T(8,128)(2,1)S(1)}, u32[]{:S(2)}, u32[]{:S(2)}) async-start(bf16[2,220,60]{1,2,0:T(8,128)(2,1)} %copy.132), calls=%async_computation.2 | async-start | bytes 131072 | tf_op jit(solution)/shard_map/all_to_all | solution.py:505
  14.4 134.0 %all-gather.2.cloned.1.call-start = ((), (), s32[]{:S(2)}) async-start(), calls=%async_computation.10 | async-start | bytes 9469952 | tf_op jit(solution)/shard_map/all_gather | solution.py:510
  31.0 349.5 %reduce-scatter.3.cloned.1.call-start = ((), (), s32[]{:S(2)}) async-start(), calls=%async_computation.11 | async-start | bytes 8355840 | tf_op jit(solution)/shard_map/reduce_scatter | solution.py:575
  31.1 44.7 %copy-start.20 = (s32[1,32]{1,0:T(1,128)S(1)}, s32[1,32]{1,0:T(1,128)}, u32[]{:S(2)}) copy-start(s32[1,32]{1,0:T(1,128)} %param.23) | copy-start | bytes 388
  31.2 50.5 %copy-start.17 = (f32[960]{0:T(1024)S(1)}, f32[960]{0:T(1024)}, u32[]{:S(2)}) copy-start(f32[960]{0:T(1024)} %param.21) | copy-start | bytes 11524
  31.4 50.6 %copy-start.12 = (bf16[256,960]{0,1:T(8,128)(2,1)S(1)}, bf16[256,960]{0,1:T(8,128)(2,1)}, u32[]{:S(2)}) copy-start(bf16[256,960]{0,1:T(8,128)(2,1)} %param.13) | copy-start | bytes 1474564
  71.5 15.2 %copy-start.4 = (bf16[64,112,128]{2,1,0:T(8,128)(2,1)}, bf16[64,112,128]{2,1,0:T(8,128)(2,1)S(1)}, u32[]{:S(2)}) copy-start(bf16[64,112,128]{2,1,0:T(8,128)(2,1)S(1)} %all_to_all.41) | copy-start | bytes 5505028
  71.5 15.2 %collective-permute-start = (bf16[2,4,4,2,112,128]{5,4,3,2,1,0:T(8,128)(2,1)S(1)}, bf16[2,4,4,2,112,128]{5,4,3,2,1,0:T(8,128)(2,1)}, u32[]{:S(2)}, u32[]{:S(2)}) collective-permute-start(bf16[2,4,4,2,112,128]{5,4,3,2,1,0:T(8,128)(2,1)S(1)} %bitcast.167), channel_id=1, source_target_pairs={{0,1},{1,0},{2,3},{3,2},{4,5},{5,4},{6,7},{7,6},{8,9},{9,8},{10,11... | collective-permute-start | bytes 5505032 | tf_op jit(solution)/shard_map/ppermute | solution.py:46
  147.8 7.9 %collective-permute-start.1 = (bf16[2048,640]{1,0:T(8,128)(2,1)}, bf16[2048,640]{1,0:T(8,128)(2,1)}, u32[]{:S(2)}, u32[]{:S(2)}) collective-permute-start(bf16[2048,640]{1,0:T(8,128)(2,1)} %bitcast.13.mine_ref), channel_id=1, source_target_pairs={{0,1},{1,0},{2,3},{3,2},{4,5},{5,4},{6,7},{7,6},{8,9},{9,8},{10,11... | collective-permute-start | bytes 7864328 | tf_op jit(solution)/shard_map/ppermute | solution.py:46
  150.8 4.7 %copy-start.18 = (f32[960]{0:T(1024)S(1)}, f32[960]{0:T(1024)}, u32[]{:S(2)}) copy-start(f32[960]{0:T(1024)} %param.22) | copy-start | bytes 11524
  151.6 30.1 %collective-permute-start.2 = (bf16[8,64,1024]{2,1,0:T(8,128)(2,1)S(1)}, bf16[8,64,1024]{2,1,0:T(8,128)(2,1)}, u32[]{:S(2)}, u32[]{:S(2)}) collective-permute-start(bf16[8,64,1024]{2,1,0:T(8,128)(2,1)S(1)} %reshape.230), channel_id=1, source_target_pairs={{0,1},{1,0},{2,3},{3,2},{4,5},{5,4},{6,7},{7,6},{8,9},{9,8},{10,11... | collective-permute-start | bytes 3145736 | tf_op jit(solution)/shard_map/ppermute | solution.py:46
  154.9 30.4 %collective-permute-start.4 = (bf16[256,1024]{1,0:T(8,128)(2,1)}, bf16[256,1024]{1,0:T(8,128)(2,1)}, u32[]{:S(2)}, u32[]{:S(2)}) collective-permute-start(bf16[256,1024]{1,0:T(8,128)(2,1)} %bitcast.151.dy_mine), channel_id=1, source_target_pairs={{0,1},{1,0},{2,3},{3,2},{4,5},{5,4},{6,7},{7,6},{8,9},{9,8},{10,11... | collective-permute-start | bytes 1572872 | tf_op jit(solution)/shard_map/ppermute | solution.py:46
  185.2 2.0 collective-permute-start.3
  210.9 2.4 copy-start.8
  210.9 2.3 collective-permute-start.6
  211.2 3.6 collective-permute-start.5
  211.8 3.0 copy-start.9
  211.8 3.0 copy-start.10
  214.8 2.9 copy-start.3
  263.5 5.1 %collective-permute-start.7 = (bf16[2048,640]{1,0:T(8,128)(2,1)}, bf16[2048,640]{1,0:T(8,128)(2,1)S(1)}, u32[]{:S(2)}, u32[]{:S(2)}) collective-permute-start(bf16[2048,640]{1,0:T(8,128)(2,1)} %get-tuple-element.37), channel_id=1, source_target_pairs={{0,1},{1,0},{2,3},{3,2},{4,5},{5,4},{6,7},{7,6},{8,9},{9,8},{10,11... | collective-permute-start | bytes 7864328 | tf_op jit(solution)/shard_map/ppermute | solution.py:46
  272.6 4.5 %copy-start.6 = (bf16[16,64,256]{2,1,0:T(8,128)(2,1)S(1)}, bf16[16,64,256]{2,1,0:T(8,128)(2,1)}, u32[]{:S(2)}) copy-start(bf16[16,64,256]{2,1,0:T(8,128)(2,1)} %copy-done.5) | copy-start | bytes 1572868
  272.6 45.4 %all-to-all-start.4 = ((bf16[8,256,640]{2,1,0:T(8,128)(2,1)}), bf16[8,256,640]{2,1,0:T(8,128)(2,1)}, u32[]{:S(2)}, u32[]{:S(2)}) async-start(bf16[8,256,640]{2,1,0:T(8,128)(2,1)} %bitcast.161), calls=%async_computation.4 | async-start | bytes 5242880 | tf_op jit(solution)/shard_map/all_to_all | solution.py:588
  279.3 52.7 %collective-permute-start.10 = (bf16[8,64,1024]{2,1,0:T(8,128)(2,1)S(1)}, bf16[8,64,1024]{2,1,0:T(8,128)(2,1)}, u32[]{:S(2)}, u32[]{:S(2)}) collective-permute-start(bf16[8,64,1024]{2,1,0:T(8,128)(2,1)S(1)} %dynamic-slice_bitcast_fusion), channel_id=1, source_target_pairs={{0,1},{1,0},{2,3},{3,2},{4,5},{5,4},{6,7},{7,6},{8,9},{9,8},{10,11... | collective-permute-start | bytes 3145736 | tf_op jit(solution)/shard_map/ppermute | solution.py:46
  321.0 11.0 %copy-start.1 = (bf16[1024,1024]{1,0:T(8,128)(2,1)S(1)}, bf16[1024,1024]{1,0:T(8,128)(2,1)}, u32[]{:S(2)}) copy-start(bf16[1024,1024]{1,0:T(8,128)(2,1)} %copy-done) | copy-start | bytes 6291460
  331.4 21.3 %collective-permute-start.8 = (bf16[2,4,4,2,112,128]{5,4,3,2,1,0:T(8,128)(2,1)}, bf16[2,4,4,2,112,128]{5,4,3,2,1,0:T(8,128)(2,1)}, u32[]{:S(2)}, u32[]{:S(2)}) collective-permute-start(bf16[2,4,4,2,112,128]{5,4,3,2,1,0:T(8,128)(2,1)} %get-tuple-element.41), channel_id=1, source_target_pairs={{0,1},{1,0},{2,3},{3,2},{4,5},{5,4},{6,7},{7,6},{8,9},{9,8},{10,11... | collective-permute-start | bytes 5505032 | tf_op jit(solution)/shard_map/ppermute | solution.py:46
  335.3 31.8 %all-to-all-start.6 = ((bf16[64,64,128]{2,1,0:T(8,128)(2,1)}), bf16[64,64,128]{2,1,0:T(8,128)(2,1)S(1)}, u32[]{:S(2)}, u32[]{:S(2)}) async-start(bf16[64,64,128]{2,1,0:T(8,128)(2,1)} %bitcast.174), calls=%async_computation.8 | async-start | bytes 2097152 | tf_op jit(solution)/shard_map/all_to_all | solution.py:583
  351.4 1.3 collective-permute-start.9
  367.1 35.5 %all-to-all-start.5 = ((bf16[64,144,128]{2,1,0:T(8,128)(2,1)}), bf16[64,144,128]{2,1,0:T(8,128)(2,1)}, u32[]{:S(2)}, u32[]{:S(2)}) async-start(bf16[64,144,128]{2,1,0:T(8,128)(2,1)} %pad_maximum_fusion), calls=%async_computation.5 | async-start | bytes 4718592 | tf_op jit(solution)/shard_map/all_to_all | solution.py:602
  373.4 36.6 %reduce-scatter.5.cloned.1.call-start = ((), (), s32[]{:S(2)}) async-start(), calls=%async_computation.12 | async-start | bytes 614400 | tf_op jit(solution)/shard_map/reduce_scatter | solution.py:576
  (7 other events, 9.1 us)
Sparse Core Ops, SparseCore 0:
  31.2 110.5 all-gather.1
  211.1 85.6 reduce-scatter.2
  380.6 29.3 reduce-scatter.4
